TPU v7x, 128 devices: a whole 4x4x4 slice. The times are simulated.
128 devices in a mesh: wide: 32 (over y, z, core), narrow: 4 (over x).
Axes of the slice: x: 4, y: 4, z: 4, core: 2. Of those that a mesh axis runs over, the one named last changes fastest.
Arguments:
- matrix: float32 [8, 2097152], P(None, ('wide', 'narrow')), may hold values from -6 to 6
- flips: int32 [2097152], P(('wide', 'narrow')), may hold values 0 or 1
- owners: int32 [131072, 1], P(('wide', 'narrow')), may hold values from 0 to 127; in each aligned block of 1024 rows (0 to 1023, 1024 to 2047, ...) at most 16 rows name the same one
- offsets: int32 [131072], P(('wide', 'narrow')), may hold values from 0 to 16383, as said below
Outputs:
- sketch: float32 [8, 131072], P(None, ('wide', 'narrow'))
- partial_gram: float32 [64, 128], P(None, ('wide', 'narrow'))
Inputs may be any that keep to these rules, and one draw needn't show every extreme that they name: `owners`: within the 1024 sampled rows of one device, no owner value appears more than 16 times, and some value appears exactly 16 times. Within the 1024 sampled rows of one device, each value of offsets // 128 appears exactly 1024 // 128 times.
All inputs are finite; a program needn't handle non-finite values. No bound on the sum of `flips` on one device may be relied on, other than what follows from the above.
Results may differ from a plain program's by a relative error of at most 0.00011.
Values sent between devices are 32-bit elements; how exact they have to be, the bound alone decides.
No kernel may reach another device: no remote copies, remote signals or barrier semaphores. Data moves between devices by JAX's collectives and lax.ppermute only.
A program may use at most 64 MiB of HBM per device.

v0:
```python
import math

import jax
import jax.numpy as jnp
from jax import lax
from jax.sharding import PartitionSpec as P


def partner_2(block, axis, stride):
    count = lax.axis_size(axis)
    route = []
    for low in range(count):
        high = low | 1 << stride
        if high != low and high < count:
            route += [(low, high), (high, low)]
    return lax.ppermute(block, axis, route)


def sylvester(count):
    left_index = lax.broadcasted_iota(jnp.int32, (count, count), 0)
    right_index = lax.broadcasted_iota(jnp.int32, (count, count), 1)
    common = jnp.bitwise_and(left_index, right_index)
    parity = jnp.zeros((count, count), jnp.int32)
    for level in range(count.bit_length() - 1):
        parity = parity + jnp.right_shift(common, level) % 2
    return (1 - 2 * (parity % 2)).astype(jnp.float32) / math.sqrt(count)


def local_transform(block):
    columns, length = block.shape
    remaining = length.bit_length() - 1
    stride = 1
    while remaining > 0:
        digit_bits = min(7, remaining)
        remaining = remaining - digit_bits
        count = 2**digit_bits
        table = sylvester(count)
        if stride == 1:
            block = jnp.dot(block.reshape(-1, count), table, precision=lax.Precision.HIGHEST)
        else:
            shaped = block.reshape(-1, count, stride)
            block = jnp.einsum("pnq,nm->pmq", shaped, table, precision=lax.Precision.HIGHEST)
        block = block.reshape(columns, length)
        stride = stride * count
    return block


def butterfly(mixed, partner, upper):
    root_half = 1.0 / math.sqrt(2.0)
    return jnp.where(upper, partner - mixed, mixed + partner) * root_half


def on_device(matrix, flips, owners, offsets):
    columns, length = matrix.shape
    signed = matrix * (2 * flips - 1).astype(jnp.float32)[None, :]
    mixed = local_transform(signed)
    wide_count = lax.axis_size("wide")
    narrow_count = lax.axis_size("narrow")
    device_count = wide_count * narrow_count
    owner_ids = owners[:, 0]
    pick_count = owner_ids.shape[0]
    for level in range(narrow_count.bit_length() - 1):
        partner = partner_2(mixed, "narrow", level)
        mixed = butterfly(mixed, partner, jnp.right_shift(lax.axis_index("narrow"), level) % 2 == 1)
    for level in range(wide_count.bit_length() - 1):
        partner = partner_2(mixed, "wide", level)
        mixed = butterfly(mixed, partner, jnp.right_shift(lax.axis_index("wide"), level) % 2 == 1)
    capacity = 2 * pick_count // device_count
    order = jnp.argsort(owner_ids, stable=True)
    sorted_ids = owner_ids[order]
    onehot = (owner_ids[:, None] == jnp.arange(device_count, dtype=jnp.int32)[None, :]).astype(
        jnp.int32
    )
    counts = jnp.sum(onehot, axis=0)
    starts = jnp.cumsum(counts) - counts
    rank = jnp.arange(pick_count, dtype=jnp.int32) - starts[sorted_ids]
    slots_sorted = sorted_ids * capacity + rank
    slots = jnp.zeros((pick_count,), jnp.int32).at[order].set(slots_sorted)
    request = jnp.zeros((device_count * capacity,), jnp.int32).at[slots].set(offsets)
    asked = lax.all_to_all(
        request.reshape(device_count, capacity),
        ("wide", "narrow"),
        split_axis=0,
        concat_axis=0,
        tiled=True,
    )
    found = mixed[:, asked.reshape(-1)]
    replied = lax.all_to_all(
        found.reshape(columns, device_count, capacity),
        ("wide", "narrow"),
        split_axis=1,
        concat_axis=1,
        tiled=True,
    )
    sketch = replied.reshape(columns, device_count * capacity)[:, slots]
    gram = jnp.dot(sketch, sketch.T, precision=lax.Precision.HIGHEST) / pick_count
    return (sketch, gram.reshape(columns * columns, 1))


def solution(mesh):
    in_specs = (
        P(None, ("wide", "narrow")),
        P(("wide", "narrow")),
        P(("wide", "narrow"), None),
        P(("wide", "narrow")),
    )
    out_specs = (P(None, ("wide", "narrow")), P(None, ("wide", "narrow")))
    return jax.shard_map(
        on_device, mesh=mesh, in_specs=in_specs, out_specs=out_specs, check_vma=False
    )
```

profile of v0, /device:TPU:1, one launch (start us, length us, event | category | flops | bytes accessed | tf_op | source)
XLA Modules:
  0.0 289.1 jit_solution(11564603507106472112)
XLA Ops:
  6.6 5.3 %copy.48 = f32[8,16384]{0,1:T(8,128)} copy(f32[8,16384]{1,0:T(8,128)S(1)} %bitcast.34) | data formatting | bytes 1048576 | tf_op jit(solution)/shard_map/reshape | solution.py:43
  11.9 5.9 %collective-permute-done = f32[8,16384]{1,0:T(8,128)S(1)} collective-permute-done((f32[8,16384]{1,0:T(8,128)S(1)}, f32[8,16384]{1,0:T(8,128)S(1)}, u32[]{:S(2)}, u32[]{:S(2)}) %collective-permute-start) | collective-permute-done | bytes 524320 | tf_op jit(solution)/shard_map/ppermute | solution.py:16
  23.0 9.9 %select_multiply_fusion.6 = f32[8,16384]{0,1:T(8,128)} fusion(f32[8,16384]{0,1:T(8,128)} %copy.48, f32[8,16384]{0,1:T(8,128)} %copy.47, pred[]{:T(512)S(6)} %eq.65), kind=kLoop, calls=%fused_computation.12 | loop fusion | flops 524288 | bytes 1572865 | tf_op jit(solution)/shard_map/mul | solution.py:50
  32.8 5.5 %copy.51 = f32[8,16384]{1,0:T(8,128)S(1)} copy(f32[8,16384]{0,1:T(8,128)} %select_multiply_fusion.6) | data formatting | bytes 1048576 | tf_op jit(solution)/shard_map/mul | solution.py:50
  41.7 10.4 %collective-permute-done.1 = f32[8,16384]{1,0:T(8,128)S(1)} collective-permute-done((f32[8,16384]{1,0:T(8,128)S(1)}, f32[8,16384]{1,0:T(8,128)S(1)}, u32[]{:S(2)}, u32[]{:S(2)}) %collective-permute-start.1) | collective-permute-done | bytes 524320 | tf_op jit(solution)/shard_map/ppermute | solution.py:16
  57.3 9.9 %select_multiply_fusion.5 = f32[8,16384]{0,1:T(8,128)} fusion(f32[8,16384]{0,1:T(8,128)} %select_multiply_fusion.6, f32[8,16384]{0,1:T(8,128)} %copy.52, pred[]{:T(512)S(6)} %eq.64), kind=kLoop, calls=%fused_computation.11 | loop fusion | flops 524288 | bytes 1572865 | tf_op jit(solution)/shard_map/mul | solution.py:50
  67.2 5.5 %copy.54 = f32[8,16384]{1,0:T(8,128)S(1)} copy(f32[8,16384]{0,1:T(8,128)} %select_multiply_fusion.5) | data formatting | bytes 1048576 | tf_op jit(solution)/shard_map/mul | solution.py:50
  82.0 9.9 %select_multiply_fusion.4 = f32[8,16384]{0,1:T(8,128)} fusion(f32[8,16384]{0,1:T(8,128)} %select_multiply_fusion.5, f32[8,16384]{0,1:T(8,128)} %copy.55, pred[]{:T(512)S(6)} %eq.63), kind=kLoop, calls=%fused_computation.10 | loop fusion | flops 524288 | bytes 1572865 | tf_op jit(solution)/shard_map/mul | solution.py:50
  91.9 5.6 %copy.57 = f32[8,16384]{1,0:T(8,128)S(1)} copy(f32[8,16384]{0,1:T(8,128)} %select_multiply_fusion.4) | data formatting | bytes 1048576 | tf_op jit(solution)/shard_map/mul | solution.py:50
  103.8 7.6 %collective-permute-done.3 = f32[8,16384]{1,0:T(8,128)S(1)} collective-permute-done((f32[8,16384]{1,0:T(8,128)S(1)}, f32[8,16384]{1,0:T(8,128)S(1)}, u32[]{:S(2)}, u32[]{:S(2)}) %collective-permute-start.3) | collective-permute-done | bytes 524320 | tf_op jit(solution)/shard_map/ppermute | solution.py:16
  116.6 9.9 %select_multiply_fusion.3 = f32[8,16384]{0,1:T(8,128)} fusion(f32[8,16384]{0,1:T(8,128)} %select_multiply_fusion.4, f32[8,16384]{0,1:T(8,128)} %copy.58, pred[]{:T(512)S(6)} %eq.62), kind=kLoop, calls=%fused_computation.9 | loop fusion | flops 524288 | bytes 1572865 | tf_op jit(solution)/shard_map/mul | solution.py:50
  126.5 5.5 %copy.60 = f32[8,16384]{1,0:T(8,128)S(1)} copy(f32[8,16384]{0,1:T(8,128)} %select_multiply_fusion.3) | data formatting | bytes 1048576 | tf_op jit(solution)/shard_map/mul | solution.py:50
  140.0 6.5 %collective-permute-done.4 = f32[8,16384]{1,0:T(8,128)S(1)} collective-permute-done((f32[8,16384]{1,0:T(8,128)S(1)}, f32[8,16384]{1,0:T(8,128)S(1)}, u32[]{:S(2)}, u32[]{:S(2)}) %collective-permute-start.4) | collective-permute-done | bytes 524320 | tf_op jit(solution)/shard_map/ppermute | solution.py:16
  151.7 9.9 %select_multiply_fusion.2 = f32[8,16384]{0,1:T(8,128)} fusion(f32[8,16384]{0,1:T(8,128)} %select_multiply_fusion.3, f32[8,16384]{0,1:T(8,128)} %copy.61, pred[]{:T(512)S(6)} %eq.61), kind=kLoop, calls=%fused_computation.8 | loop fusion | flops 524288 | bytes 1572865 | tf_op jit(solution)/shard_map/mul | solution.py:50
  161.5 5.5 %copy.63 = f32[8,16384]{1,0:T(8,128)S(1)} copy(f32[8,16384]{0,1:T(8,128)} %select_multiply_fusion.2) | data formatting | bytes 1048576 | tf_op jit(solution)/shard_map/mul | solution.py:50
  169.1 6.6 %gather_fusion.1 = s32[1024]{0:T(1024)S(1)} fusion(s32[128]{0:T(128)S(1)} %sub.46, s32[1024]{0:T(1024)S(1)} %broadcast_clamp_fusion.2), kind=kCustom, calls=%fused_computation.1 | custom fusion | bytes 12288 | tf_op jit(solution)/shard_map/gather | solution.py:76
  185.2 11.2 %all-to-all-start = ((s32[128,1,16]{2,1,0:T(1,128)}), s32[128,1,16]{2,1,0:T(1,128)S(1)}, u32[]{:S(2)}, u32[]{:S(2)}) async-start(s32[128,1,16]{2,1,0:T(1,128)} %bitcast.8), calls=%async_computation | async-start | bytes 131072 | tf_op jit(solution)/shard_map/all_to_all | solution.py:80
  196.4 9.9 %all-to-all-done = s32[128,1,16]{2,1,0:T(1,128)S(1)} async-done(((s32[128,1,16]{2,1,0:T(1,128)}), s32[128,1,16]{2,1,0:T(1,128)S(1)}, u32[]{:S(2)}, u32[]{:S(2)}) %all-to-all-start) | async-done | bytes 8224 | tf_op jit(solution)/shard_map/all_to_all | solution.py:80
  213.0 9.9 %select_multiply_fusion.1 = f32[8,16384]{0,1:T(8,128)} fusion(f32[8,16384]{0,1:T(8,128)} %select_multiply_fusion.2, f32[8,16384]{0,1:T(8,128)} %copy.64, pred[]{:T(512)S(6)} %eq.60), kind=kLoop, calls=%fused_computation.7 | loop fusion | flops 524288 | bytes 1572865 | tf_op jit(solution)/shard_map/mul | solution.py:50
  222.9 5.5 %copy.66 = f32[8,16384]{1,0:T(8,128)S(1)} copy(f32[8,16384]{0,1:T(8,128)} %select_multiply_fusion.1) | data formatting | bytes 1048576 | tf_op jit(solution)/shard_map/mul | solution.py:50
  229.0 14.2 %collective-permute-done.6 = f32[8,16384]{1,0:T(8,128)S(1)} collective-permute-done((f32[8,16384]{1,0:T(8,128)S(1)}, f32[8,16384]{1,0:T(8,128)S(1)}, u32[]{:S(2)}, u32[]{:S(2)}) %collective-permute-start.6) | collective-permute-done | bytes 524320 | tf_op jit(solution)/shard_map/ppermute | solution.py:16
  248.4 9.9 %select_multiply_fusion = f32[8,16384]{0,1:T(8,128)} fusion(f32[8,16384]{0,1:T(8,128)} %select_multiply_fusion.1, f32[8,16384]{0,1:T(8,128)} %copy.67, pred[]{:T(512)S(6)} %eq.59), kind=kLoop, calls=%fused_computation.6 | loop fusion | flops 524288 | bytes 1572865 | tf_op jit(solution)/shard_map/mul | solution.py:50
  258.2 8.8 %gather_fusion.2 = f32[2048,8]{1,0:T(8,128)S(1)} fusion(f32[8,16384]{0,1:T(8,128)} %select_multiply_fusion, s32[2048]{0:T(1024)S(1)} %broadcast_clamp_fusion), kind=kCustom, calls=%fused_computation.2 | custom fusion | bytes 139264 | tf_op jit(solution)/shard_map/gather | solution.py:87
  267.6 14.4 %all_to_all.14 = f32[128,1,128]{2,1,0:T(1,128)S(1)} all-to-all(f32[128,1,128]{2,1,0:T(1,128)S(1)} %reshape.170), channel_id=1, replica_groups=mesh['wide'=32,'narrow'=4] {'wide','narrow'}, dimensions={0} | all-to-all | bytes 131072 | tf_op jit(solution)/shard_map/all_to_all | solution.py:88
  (54 shorter events, 85.1 us)
Async XLA Ops:
  4.5 13.3 %collective-permute-start = (f32[8,16384]{1,0:T(8,128)S(1)}, f32[8,16384]{1,0:T(8,128)S(1)}, u32[]{:S(2)}, u32[]{:S(2)}) collective-permute-start(f32[8,16384]{1,0:T(8,128)S(1)} %bitcast.33), channel_id=1, source_target_pairs={{0,1},{1,0},{2,3},{3,2},{4,5},{5,4},{6,7},{7,6},{8,9},{9,8},{10,11... | collective-permute-start | bytes 1572872 | tf_op jit(solution)/shard_map/ppermute | solution.py:16
  38.4 13.7 %collective-permute-start.1 = (f32[8,16384]{1,0:T(8,128)S(1)}, f32[8,16384]{1,0:T(8,128)S(1)}, u32[]{:S(2)}, u32[]{:S(2)}) collective-permute-start(f32[8,16384]{1,0:T(8,128)S(1)} %copy.51), channel_id=1, source_target_pairs={{0,2},{2,0},{1,3},{3,1},{4,6},{6,4},{5,7},{7,5},{8,10},{10,8},{9,1... | collective-permute-start | bytes 1572872 | tf_op jit(solution)/shard_map/ppermute | solution.py:16
  72.8 4.1 %collective-permute-start.2 = (f32[8,16384]{1,0:T(8,128)S(1)}, f32[8,16384]{1,0:T(8,128)S(1)}, u32[]{:S(2)}, u32[]{:S(2)}) collective-permute-start(f32[8,16384]{1,0:T(8,128)S(1)} %copy.54), channel_id=1, source_target_pairs={{0,4},{4,0},{8,12},{12,8},{16,20},{20,16},{24,28},{28,24},{32,36},... | collective-permute-start | bytes 1572872 | tf_op jit(solution)/shard_map/ppermute | solution.py:16
  91.9 7.5 %copy-start = (s32[1024,1]{0,1:T(1,128)S(1)}, s32[1024,1]{0,1:T(1,128)}, u32[]{:S(2)}) copy-start(s32[1024,1]{0,1:T(1,128)} %param.6) | copy-start | bytes 12292
  97.5 13.9 %collective-permute-start.3 = (f32[8,16384]{1,0:T(8,128)S(1)}, f32[8,16384]{1,0:T(8,128)S(1)}, u32[]{:S(2)}, u32[]{:S(2)}) collective-permute-start(f32[8,16384]{1,0:T(8,128)S(1)} %copy.57), channel_id=1, source_target_pairs={{0,8},{8,0},{4,12},{12,4},{16,24},{24,16},{20,28},{28,20},{32,40},... | collective-permute-start | bytes 1572872 | tf_op jit(solution)/shard_map/ppermute | solution.py:16
  132.0 14.4 %collective-permute-start.4 = (f32[8,16384]{1,0:T(8,128)S(1)}, f32[8,16384]{1,0:T(8,128)S(1)}, u32[]{:S(2)}, u32[]{:S(2)}) collective-permute-start(f32[8,16384]{1,0:T(8,128)S(1)} %copy.60), channel_id=1, source_target_pairs={{0,16},{16,0},{4,20},{20,4},{8,24},{24,8},{12,28},{28,12},{32,48},... | collective-permute-start | bytes 1572872 | tf_op jit(solution)/shard_map/ppermute | solution.py:16
  167.1 40.6 %collective-permute-start.5 = (f32[8,16384]{1,0:T(8,128)S(1)}, f32[8,16384]{1,0:T(8,128)S(1)}, u32[]{:S(2)}, u32[]{:S(2)}) collective-permute-start(f32[8,16384]{1,0:T(8,128)S(1)} %copy.63), channel_id=1, source_target_pairs={{0,32},{32,0},{4,36},{36,4},{8,40},{40,8},{12,44},{44,12},{16,48},... | collective-permute-start | bytes 1572872 | tf_op jit(solution)/shard_map/ppermute | solution.py:16
  185.2 21.1 %all-to-all-start = ((s32[128,1,16]{2,1,0:T(1,128)}), s32[128,1,16]{2,1,0:T(1,128)S(1)}, u32[]{:S(2)}, u32[]{:S(2)}) async-start(s32[128,1,16]{2,1,0:T(1,128)} %bitcast.8), calls=%async_computation | async-start | bytes 131072 | tf_op jit(solution)/shard_map/all_to_all | solution.py:80
  228.4 14.7 %collective-permute-start.6 = (f32[8,16384]{1,0:T(8,128)S(1)}, f32[8,16384]{1,0:T(8,128)S(1)}, u32[]{:S(2)}, u32[]{:S(2)}) collective-permute-start(f32[8,16384]{1,0:T(8,128)S(1)} %copy.66), channel_id=1, source_target_pairs={{0,64},{64,0},{4,68},{68,4},{8,72},{72,8},{12,76},{76,12},{16,80},... | collective-permute-start | bytes 1572872 | tf_op jit(solution)/shard_map/ppermute | solution.py:16
where the time goes:
time: 290 us; the launch traced here: 289 us
  local copies, waits for them, and re-layouts  111 us (38%)
  other arithmetic  77.6 us (27%)
  waiting for transfers between devices  56 us (19%)
  starting transfers between devices  26.3 us (9%)
  blocking collectives  14.4 us (5%)
    mul x7, other arithmetic, butterfly(): return jnp.where(upper, partner - mixed, mixed + partner) * root_half  69.1 us
    ppermute x7, waiting for transfers between devices, partner_2(): return lax.ppermute(block, axis, route)  46.1 us
    ppermute x7, local copies, waits for them, and re-layouts, partner_2(): return lax.ppermute(block, axis, route)  36.6 us
    mul x6, local copies, waits for them, and re-layouts, butterfly(): return jnp.where(upper, partner - mixed, mixed + partner) * root_half  33.3 us
    ppermute x7, starting transfers between devices, partner_2(): return lax.ppermute(block, axis, route)  15.1 us
    all_to_all x1, blocking collectives, on_device(): lax.all_to_all(found.reshape(columns, device_count, capacity), ('wide', '...  14.4 us
    all_to_all x1, starting transfers between devices, on_device(): lax.all_to_all(request.reshape(device_count, capacity), ('wide', 'narrow'...  11.2 us
    all_to_all x1, waiting for transfers between devices, on_device(): lax.all_to_all(request.reshape(device_count, capacity), ('wide', 'narrow'...  9.87 us
  transfers between devices with their start and end apart: 8, of which 7 were waited for; matrix products, arithmetic and copies ran while one was open for 11% of the time, Pallas kernels for 0%

commit v1 on v0

v1 whole, which is shorter than its diff:
```python
import functools
import math

import jax
import jax.numpy as jnp
from jax import lax
from jax.experimental import pallas as pl
from jax.experimental.pallas import tpu as pltpu
from jax.sharding import PartitionSpec as P

LANES = 128
SLOTS = 8
COLS = 8
CHUNK = COLS + 1
PICKS = LANES * SLOTS
VMEM = pl.BlockSpec(memory_space=pltpu.VMEM)
ACROSS = ("wide", "narrow")


def walsh(tiles):
    span = 1
    while span < len(tiles):
        out = list(tiles)
        for i in range(len(tiles)):
            if not i & span:
                out[i] = tiles[i] + tiles[i | span]
                out[i | span] = tiles[i] - tiles[i | span]
        tiles = out
        span *= 2
    return tiles


def one_hot(section):
    rows = lax.broadcasted_iota(jnp.int32, (LANES, section.shape[1]), 0)
    return rows == section


def split(values):
    high = values.astype(jnp.bfloat16)
    return high, (values - high.astype(jnp.float32)).astype(jnp.bfloat16)


def send_kernel(matrix, flips, owners, offsets, message, rank_out, signs, mid):
    place = offsets[...]
    section = lax.shift_right_logical(place, 7)
    hot = one_hot(section).astype(jnp.float32)
    before = lax.broadcasted_iota(jnp.int32, (LANES, LANES), 0) < lax.broadcasted_iota(jnp.int32, (LANES, LANES), 1)
    table = jnp.concatenate([before.astype(jnp.float32), jnp.ones((LANES, LANES), jnp.float32)], axis=1)
    table = table.astype(jnp.bfloat16)
    carry = jnp.zeros((LANES, LANES), jnp.float32)
    ranks = []
    for t in range(SLOTS):
        part = hot[:, t * LANES : (t + 1) * LANES]
        sums = jnp.dot(part.astype(jnp.bfloat16), table, preferred_element_type=jnp.float32)
        ranks.append(jnp.sum(part * (sums[:, :LANES] + carry), axis=0, keepdims=True))
        carry = carry + sums[:, LANES:]
    rank = jnp.concatenate(ranks, axis=1)
    rank_out[...] = rank.astype(jnp.int32)
    slot = lax.broadcasted_iota(jnp.int32, (SLOTS, PICKS), 0) == rank.astype(jnp.int32)
    low = (place & (LANES - 1)).astype(jnp.float32)
    wanted = jnp.concatenate(
        [jnp.where(slot, owners[...].astype(jnp.float32), 0.0), jnp.where(slot, low, 0.0)], axis=0
    )
    found = lax.dot_general(
        hot.astype(jnp.bfloat16),
        wanted.astype(jnp.bfloat16),
        (((1,), (1,)), ((), ())),
        preferred_element_type=jnp.float32,
    )
    rows = lax.broadcasted_iota(jnp.int32, (LANES, SLOTS), 0).astype(jnp.float32) * float(LANES)
    rows = found[:, :SLOTS] * float(LANES * LANES) + rows + found[:, SLOTS:]
    rows = jnp.concatenate([rows, jnp.zeros((LANES, LANES - SLOTS), jnp.float32)], axis=1)
    message[pl.ds(COLS, LANES, stride=CHUNK), :] = rows

    scale = 1.0 / math.sqrt(float(LANES) ** 3)
    signs[...] = jnp.where(flips[...] == 1, scale, -scale)
    for j in range(8):
        tiles = []
        for i in range(16):
            f = i * 8 + j
            tiles.append(matrix[:, f * LANES : (f + 1) * LANES] * signs[f : f + 1, :])
        for i, tile in enumerate(walsh(tiles)):
            mid[i * 8 + j] = tile
    for i in range(16):
        for j, tile in enumerate(walsh([mid[i * 8 + j] for j in range(8)])):
            message[pl.ds((i * 8 + j) * CHUNK, COLS), :] = tile


def sign_table(index):
    bit = lambda b: 1.0 - 2.0 * (lax.shift_right_logical(index, b) & 1).astype(jnp.float32)
    row = lax.broadcasted_iota(jnp.int32, (8, index.shape[1]), 0)
    block = jnp.ones((8, index.shape[1]), jnp.float32)
    for b in range(3):
        block = block * jnp.where(lax.shift_right_logical(row, b) & 1 == 1, bit(b), 1.0)
    blocks = [block]
    for b in range(3, 7):
        factor = bit(b)
        blocks = blocks + [block * factor for block in blocks]
    return jnp.concatenate(blocks, axis=0)


def answer_kernel(message, reply, left, right, signs):
    wanted = message[pl.ds(COLS, LANES, stride=CHUNK), :]
    wanted = wanted.T[:SLOTS, :].astype(jnp.int32)
    for r in range(SLOTS):
        index = wanted[r : r + 1, :]
        cut = slice(r * LANES, (r + 1) * LANES)
        table = sign_table(index & (LANES - 1)).astype(jnp.bfloat16)
        right[:LANES, cut] = table
        right[LANES:, cut] = table
        signs[:, cut] = sign_table(lax.shift_right_logical(index, 14))
    for pair in range(LANES // 2):
        tile = jnp.concatenate(
            [message[pl.ds(d * CHUNK, COLS), :] for d in (2 * pair, 2 * pair + 1)], axis=0
        )
        high, low = split(tile)
        left[pl.ds(pair * 16, 16), :LANES] = high
        left[pl.ds(pair * 16, 16), LANES:] = low
    answers = []
    width = 256
    for n in range(PICKS // width):
        cut = slice(n * width, (n + 1) * width)
        total = jnp.zeros((COLS, width), jnp.float32)
        for m in range(4):
            part = jnp.dot(left[m * 256 : (m + 1) * 256, :], right[:, cut], preferred_element_type=jnp.float32)
            for d in range(32):
                total = total + part[d * COLS : (d + 1) * COLS, :] * signs[m * 32 + d : m * 32 + d + 1, cut]
        answers += [total[:, :LANES], total[:, LANES:]]
    answers.append(jnp.zeros((LANES - SLOTS * COLS, LANES), jnp.float32))
    reply[...] = jnp.concatenate(answers, axis=0).T


def finish_kernel(reply, offsets, rank, sketch, gram):
    section = lax.shift_right_logical(offsets[...], 7)
    hot = one_hot(section).astype(jnp.float32).astype(jnp.bfloat16)
    high, low = split(reply[...].T[: SLOTS * COLS, :])
    parts = jnp.dot(high, hot, preferred_element_type=jnp.float32) + jnp.dot(
        low, hot, preferred_element_type=jnp.float32
    )
    place = rank[...]
    total = jnp.zeros((COLS, PICKS), jnp.float32)
    for r in range(SLOTS):
        total = total + jnp.where(place == r, parts[r * COLS : (r + 1) * COLS, :], 0.0)
    sketch[...] = total
    products = []
    for a in range(COLS):
        product = total * total[a : a + 1, :]
        products.append(sum(product[:, t * LANES : (t + 1) * LANES] for t in range(SLOTS)))
    products = jnp.concatenate(products + [jnp.zeros((LANES - COLS * COLS, LANES), jnp.float32)], axis=0)
    gram[...] = jnp.sum(products.T, axis=0, keepdims=True) * (1.0 / PICKS)


def on_device(matrix, flips, owners, offsets):
    f32 = jnp.float32
    offsets = offsets.reshape(1, PICKS)
    message, rank = pl.pallas_call(
        send_kernel,
        name="transform_sections",
        out_shape=(
            jax.ShapeDtypeStruct((LANES * CHUNK, LANES), f32),
            jax.ShapeDtypeStruct((1, PICKS), jnp.int32),
        ),
        in_specs=[VMEM] * 4,
        out_specs=(VMEM, VMEM),
        scratch_shapes=[pltpu.VMEM((LANES, LANES), f32), pltpu.VMEM((LANES, COLS, LANES), f32)],
        compiler_params=pltpu.CompilerParams(vmem_limit_bytes=32 * 2**20),
    )(matrix, flips.reshape(LANES, LANES), owners.reshape(1, PICKS), offsets)
    message = lax.all_to_all(
        message.reshape(LANES, 1, CHUNK * LANES), ACROSS, split_axis=0, concat_axis=0, tiled=True
    ).reshape(LANES * CHUNK, LANES)
    reply = pl.pallas_call(
        answer_kernel,
        name="answer",
        out_shape=jax.ShapeDtypeStruct((LANES, LANES), f32),
        in_specs=[VMEM],
        out_specs=VMEM,
        scratch_shapes=[
            pltpu.VMEM((LANES * COLS, 2 * LANES), jnp.bfloat16),
            pltpu.VMEM((2 * LANES, PICKS), jnp.bfloat16),
            pltpu.VMEM((LANES, PICKS), f32),
        ],
        compiler_params=pltpu.CompilerParams(vmem_limit_bytes=32 * 2**20),
    )(message)
    reply = lax.all_to_all(
        reply.reshape(LANES, 1, LANES), ACROSS, split_axis=0, concat_axis=0, tiled=True
    ).reshape(LANES, LANES)
    sketch, gram = pl.pallas_call(
        finish_kernel,
        name="finish",
        out_shape=(jax.ShapeDtypeStruct((COLS, PICKS), f32), jax.ShapeDtypeStruct((1, LANES), f32)),
        in_specs=[VMEM] * 3,
        out_specs=(VMEM, VMEM),
        compiler_params=pltpu.CompilerParams(vmem_limit_bytes=32 * 2**20),
    )(reply, offsets, rank)
    return sketch, gram[:, : COLS * COLS].reshape(COLS * COLS, 1)


def solution(mesh):
    in_specs = (P(None, ACROSS), P(ACROSS), P(ACROSS, None), P(ACROSS))
    out_specs = (P(None, ACROSS), P(None, ACROSS))
    return jax.shard_map(on_device, mesh=mesh, in_specs=in_specs, out_specs=out_specs, check_vma=False)
```

time: 290 us -> 46.5 us (0.16)
  local copies, waits for them, and re-layouts: 111 us -> 3.76 us
  other arithmetic: 77.6 us -> 0 us
  waiting for transfers between devices: 56 us -> 0 us
  starting transfers between devices: 26.3 us -> 0 us
  blocking collectives: 14.4 us -> 39.3 us
    mul x7 -> x0, other arithmetic: 69.1 us -> none  [butterfly(): return jnp.where(upper, partner - mixed, mixed + partner) * root_half]
    ppermute x7 -> x0, waiting for transfers between devices: 46.1 us -> none  [partner_2(): return lax.ppermute(block, axis, route)]
    ppermute x7 -> x0, local copies, waits for them, and re-layouts: 36.6 us -> none  [partner_2(): return lax.ppermute(block, axis, route)]
    mul x6 -> x0, local copies, waits for them, and re-layouts: 33.3 us -> none  [butterfly(): return jnp.where(upper, partner - mixed, mixed + partner) * root_half]
    all_to_all x1 -> x2, blocking collectives: 14.4 us -> 39.3 us  [the longest x1 26.1 us: on_device(): lax.all_to_all(message.reshape(LANES, 1, CHUNK * LANES), ACROSS, split_ax...]
    gather x4 -> x0, local copies, waits for them, and re-layouts: 22.7 us -> none  [the longest x1 8.84 us: on_device(): found = mixed[:, asked.reshape(-1)]]
    ppermute x7 -> x0, starting transfers between devices: 15.1 us -> none  [partner_2(): return lax.ppermute(block, axis, route)]
    all_to_all x1 -> x0, starting transfers between devices: 11.2 us -> none  [on_device(): lax.all_to_all(request.reshape(device_count, capacity), ('wide', 'narrow'...]
  transfers between devices with their start and end apart: 8 -> 0, of which waited for: 7 -> 0; matrix products, arithmetic and copies ran while one was open for 11% -> 0% of each run, Pallas kernels for 0% -> 0%
where the time goes in v1:
time: 46.5 us; the launch traced here: 46.2 us
  blocking collectives  39.3 us (85%)
  local copies, waits for them, and re-layouts  3.76 us (8%)
  Pallas kernels  2.53 us (5%)
  between operations  0.65 us (1%)
    all_to_all x1, blocking collectives, on_device(): lax.all_to_all(message.reshape(LANES, 1, CHUNK * LANES), ACROSS, split_ax...  26.1 us
    all_to_all x1, blocking collectives, on_device(): lax.all_to_all(reply.reshape(LANES, 1, LANES), ACROSS, split_axis=0, conc...  13.2 us
    unnamed x8, local copies, waits for them, and re-layouts  3.25 us
    pallas_call x1, Pallas kernels, on_device(): pl.pallas_call(answer_kernel, name='answer', out_shape=jax.ShapeDtypeStru...  0.94 us
    pallas_call x1, Pallas kernels, on_device(): pl.pallas_call(finish_kernel, name='finish', out_shape=(jax.ShapeDtypeStr...  0.94 us

profile of v1, /device:TPU:1, one launch (start us, length us, event | category | flops | bytes accessed | tf_op | source)
XLA Modules:
  0.0 46.2 jit_solution(603348926518073744)
XLA Ops:
  0.6 0.0 copy-start.2
  0.6 0.7 %copy-done.2 = s32[1024]{0:T(1024)S(1)} copy-done((s32[1024]{0:T(1024)S(1)}, s32[1024]{0:T(1024)}, u32[]{:S(2)}) %copy-start.2) | copy-done | bytes 4120
  1.3 0.0 copy-start
  1.3 1.0 %copy-done = f32[8,16384]{1,0:T(8,128)S(1)} copy-done((f32[8,16384]{1,0:T(8,128)S(1)}, f32[8,16384]{1,0:T(8,128)}, u32[]{:S(2)}) %copy-start) | copy-done | bytes 524312
  2.4 0.0 copy-start.1
  2.4 0.8 %copy-done.1 = s32[16384]{0:T(1024)S(1)} copy-done((s32[16384]{0:T(1024)S(1)}, s32[16384]{0:T(1024)}, u32[]{:S(2)}) %copy-start.1) | copy-done | bytes 65560
  3.2 0.0 copy-start.3
  3.2 0.7 %copy-done.3 = s32[1024,1]{0,1:T(1,128)S(1)} copy-done((s32[1024,1]{0,1:T(1,128)S(1)}, s32[1024,1]{0,1:T(1,128)}, u32[]{:S(2)}) %copy-start.3) | copy-done | bytes 4120
  3.9 0.6 %transform_sections.1 = (f32[1152,128]{1,0:T(8,128)S(1)}, s32[1,1024]{1,0:T(1,128)S(1)}) custom-call(f32[8,16384]{1,0:T(8,128)S(1)} %copy-done, s32[128,128]{1,0:T(8,128)S(1)} %bitcast.15, s32[1,1024]{1,0:T(1,128)S(1)} %bitcast.18, s32[1,1024]{1,0:T(1,128)S(1)} %bitcast.16), custom_call_target="tpu_custom_call" | custom-call | tf_op jit(solution)/shard_map/transform_sections/pallas_call | solution.py:156
  4.5 26.1 %all_to_all.10 = f32[128,1,1152]{2,1,0:T(1,128)S(1)} all-to-all(f32[128,1,1152]{2,1,0:T(1,128)S(1)} %bitcast.12), channel_id=1, replica_groups=mesh['wide'=32,'narrow'=4] {'wide','narrow'}, dimensions={0} | all-to-all | bytes 1179648 | tf_op jit(solution)/shard_map/all_to_all | solution.py:168
  30.7 0.9 %answer.1 = f32[128,128]{1,0:T(8,128)S(1)} custom-call(f32[1152,128]{1,0:T(8,128)S(1)} %bitcast.11), custom_call_target="tpu_custom_call" | custom-call | tf_op jit(solution)/shard_map/answer/pallas_call | solution.py:171
  31.6 13.2 %all_to_all.11 = f32[128,1,128]{2,1,0:T(1,128)S(1)} all-to-all(f32[128,1,128]{2,1,0:T(1,128)S(1)} %bitcast.13), channel_id=1, replica_groups=mesh['wide'=32,'narrow'=4] {'wide','narrow'}, dimensions={0} | all-to-all | bytes 131072 | tf_op jit(solution)/shard_map/all_to_all | solution.py:184
  44.8 0.9 %finish.1 = (f32[8,1024]{1,0:T(8,128)}, f32[1,128]{1,0:T(1,128)S(1)}) custom-call(f32[128,128]{1,0:T(8,128)S(1)} %bitcast.14, s32[1,1024]{1,0:T(1,128)S(1)} %bitcast.17, s32[1,1024]{1,0:T(1,128)S(1)} %get-tuple-element.7.rank), custom_call_target="tpu_custom_call" | custom-call | tf_op jit(solution)/shard_map/finish/pallas_call | solution.py:187
  45.7 0.5 %slice_bitcast_fusion = f32[64,1]{0,1:T(1,128)} fusion(f32[1,128]{1,0:T(1,128)S(1)} %get-tuple-element.9), kind=kLoop, calls=%fused_computation | loop fusion | bytes 512 | tf_op jit(solution)/shard_map/reshape | solution.py:195
Async XLA Ops:
  0.6 0.7 %copy-start.2 = (s32[1024]{0:T(1024)S(1)}, s32[1024]{0:T(1024)}, u32[]{:S(2)}) copy-start(s32[1024]{0:T(1024)} %param.7) | copy-start | bytes 12292
  1.3 1.0 %copy-start = (f32[8,16384]{1,0:T(8,128)S(1)}, f32[8,16384]{1,0:T(8,128)}, u32[]{:S(2)}) copy-start(f32[8,16384]{1,0:T(8,128)} %matrix.1) | copy-start | bytes 1572868
  2.4 0.8 %copy-start.1 = (s32[16384]{0:T(1024)S(1)}, s32[16384]{0:T(1024)}, u32[]{:S(2)}) copy-start(s32[16384]{0:T(1024)} %param.5) | copy-start | bytes 196612
  3.2 0.7 %copy-start.3 = (s32[1024,1]{0,1:T(1,128)S(1)}, s32[1024,1]{0,1:T(1,128)}, u32[]{:S(2)}) copy-start(s32[1024,1]{0,1:T(1,128)} %param.6) | copy-start | bytes 12292

commit v2 on v1

--- a/solution.py
+++ b/solution.py
@@ -1,4 +1,3 @@
-import functools
 import math
 
 import jax
@@ -13,7 +12,9 @@
 COLS = 8
 CHUNK = COLS + 1
 PICKS = LANES * SLOTS
+PIECES = 4
 VMEM = pl.BlockSpec(memory_space=pltpu.VMEM)
+HBM = pl.BlockSpec(memory_space=pltpu.HBM)
 ACROSS = ("wide", "narrow")
 
 
@@ -40,7 +41,23 @@
     return high, (values - high.astype(jnp.float32)).astype(jnp.bfloat16)
 
 
-def send_kernel(matrix, flips, owners, offsets, message, rank_out, signs, mid):
+def send_kernel(
+    matrix_hbm, flips_hbm, owners_hbm, offsets_hbm, message, slots_out, matrix, flips, owners, offsets, mid, arrived
+):
+    copies = [
+        pltpu.make_async_copy(source, target, arrived.at[i])
+        for i, (source, target) in enumerate(
+            ((offsets_hbm, offsets), (owners_hbm, owners), (flips_hbm, flips))
+        )
+    ]
+    width = matrix.shape[1] // PIECES
+    for p in range(PIECES):
+        cut = pl.ds(p * width, width)
+        copies.append(pltpu.make_async_copy(matrix_hbm.at[:, cut], matrix.at[:, cut], arrived.at[3 + p]))
+    for copy in copies:
+        copy.start()
+
+    copies[0].wait()
     place = offsets[...]
     section = lax.shift_right_logical(place, 7)
     hot = one_hot(section).astype(jnp.float32)
@@ -54,10 +71,11 @@
         sums = jnp.dot(part.astype(jnp.bfloat16), table, preferred_element_type=jnp.float32)
         ranks.append(jnp.sum(part * (sums[:, :LANES] + carry), axis=0, keepdims=True))
         carry = carry + sums[:, LANES:]
-    rank = jnp.concatenate(ranks, axis=1)
-    rank_out[...] = rank.astype(jnp.int32)
-    slot = lax.broadcasted_iota(jnp.int32, (SLOTS, PICKS), 0) == rank.astype(jnp.int32)
+    rank = jnp.concatenate(ranks, axis=1).astype(jnp.int32)
+    slots_out[...] = section * SLOTS + rank
+    slot = lax.broadcasted_iota(jnp.int32, (SLOTS, PICKS), 0) == rank
     low = (place & (LANES - 1)).astype(jnp.float32)
+    copies[1].wait()
     wanted = jnp.concatenate(
         [jnp.where(slot, owners[...].astype(jnp.float32), 0.0), jnp.where(slot, low, 0.0)], axis=0
     )
@@ -73,16 +91,18 @@
     message[pl.ds(COLS, LANES, stride=CHUNK), :] = rows
 
     scale = 1.0 / math.sqrt(float(LANES) ** 3)
-    signs[...] = jnp.where(flips[...] == 1, scale, -scale)
+    copies[2].wait()
+    signs = jnp.where(flips[...] == 1, scale, -scale)
+    for i in range(16):
+        if i * PIECES % 16 == 0:
+            copies[3 + i * PIECES // 16].wait()
+        tiles = []
+        for f in range(i * 8, i * 8 + 8):
+            tiles.append(matrix[:, f * LANES : (f + 1) * LANES] * signs[f : f + 1, :])
+        for j, tile in enumerate(walsh(tiles)):
+            mid[i * 8 + j] = tile
     for j in range(8):
-        tiles = []
-        for i in range(16):
-            f = i * 8 + j
-            tiles.append(matrix[:, f * LANES : (f + 1) * LANES] * signs[f : f + 1, :])
-        for i, tile in enumerate(walsh(tiles)):
-            mid[i * 8 + j] = tile
-    for i in range(16):
-        for j, tile in enumerate(walsh([mid[i * 8 + j] for j in range(8)])):
+        for i, tile in enumerate(walsh([mid[i * 8 + j] for i in range(16)])):
             message[pl.ds((i * 8 + j) * CHUNK, COLS), :] = tile
 
 
@@ -130,41 +150,65 @@
     reply[...] = jnp.concatenate(answers, axis=0).T
 
 
-def finish_kernel(reply, offsets, rank, sketch, gram):
-    section = lax.shift_right_logical(offsets[...], 7)
-    hot = one_hot(section).astype(jnp.float32).astype(jnp.bfloat16)
+def finish_kernel(reply, slots, sketch_hbm, gram_hbm, sketch, gram, sent):
+    place = slots[...]
+    hot = one_hot(lax.shift_right_logical(place, 3)).astype(jnp.float32).astype(jnp.bfloat16)
     high, low = split(reply[...].T[: SLOTS * COLS, :])
     parts = jnp.dot(high, hot, preferred_element_type=jnp.float32) + jnp.dot(
         low, hot, preferred_element_type=jnp.float32
     )
-    place = rank[...]
+    place = place & (SLOTS - 1)
     total = jnp.zeros((COLS, PICKS), jnp.float32)
     for r in range(SLOTS):
         total = total + jnp.where(place == r, parts[r * COLS : (r + 1) * COLS, :], 0.0)
     sketch[...] = total
+    first = pltpu.make_async_copy(sketch, sketch_hbm, sent.at[0])
+    first.start()
     products = []
     for a in range(COLS):
         product = total * total[a : a + 1, :]
         products.append(sum(product[:, t * LANES : (t + 1) * LANES] for t in range(SLOTS)))
     products = jnp.concatenate(products + [jnp.zeros((LANES - COLS * COLS, LANES), jnp.float32)], axis=0)
-    gram[...] = jnp.sum(products.T, axis=0, keepdims=True) * (1.0 / PICKS)
+    products = jnp.sum(products.T, axis=0, keepdims=True) * (1.0 / PICKS)
+    gram[...] = products[:, : COLS * COLS]
+    second = pltpu.make_async_copy(gram, gram_hbm, sent.at[1])
+    second.start()
+    first.wait()
+    second.wait()
 
 
 def on_device(matrix, flips, owners, offsets):
-    f32 = jnp.float32
-    offsets = offsets.reshape(1, PICKS)
-    message, rank = pl.pallas_call(
+    f32, i32 = jnp.float32, jnp.int32
+    params = pltpu.CompilerParams(vmem_limit_bytes=32 * 2**20)
+    message, slots = pl.pallas_call(
         send_kernel,
         name="transform_sections",
         out_shape=(
             jax.ShapeDtypeStruct((LANES * CHUNK, LANES), f32),
-            jax.ShapeDtypeStruct((1, PICKS), jnp.int32),
+            jax.ShapeDtypeStruct((1, PICKS), i32),
         ),
-        in_specs=[VMEM] * 4,
+        in_specs=[HBM] * 4,
         out_specs=(VMEM, VMEM),
-        scratch_shapes=[pltpu.VMEM((LANES, LANES), f32), pltpu.VMEM((LANES, COLS, LANES), f32)],
-        compiler_params=pltpu.CompilerParams(vmem_limit_bytes=32 * 2**20),
-    )(matrix, flips.reshape(LANES, LANES), owners.reshape(1, PICKS), offsets)
+        scratch_shapes=[
+            pltpu.VMEM((COLS, LANES * LANES), f32),
+            pltpu.VMEM((LANES, LANES), i32),
+            pltpu.VMEM((1, PICKS), i32),
+            pltpu.VMEM((1, PICKS), i32),
+            pltpu.VMEM((LANES, COLS, LANES), f32),
+            pltpu.SemaphoreType.DMA((3 + PIECES,)),
+        ],
+        compiler_params=params,
+    )(
+        *(
+            pltpu.with_memory_space_constraint(operand, pltpu.HBM)
+            for operand in (
+                matrix,
+                flips.reshape(LANES, LANES),
+                owners.reshape(1, PICKS),
+                offsets.reshape(1, PICKS),
+            )
+        )
+    )
     message = lax.all_to_all(
         message.reshape(LANES, 1, CHUNK * LANES), ACROSS, split_axis=0, concat_axis=0, tiled=True
     ).reshape(LANES * CHUNK, LANES)
@@ -179,7 +223,7 @@
             pltpu.VMEM((2 * LANES, PICKS), jnp.bfloat16),
             pltpu.VMEM((LANES, PICKS), f32),
         ],
-        compiler_params=pltpu.CompilerParams(vmem_limit_bytes=32 * 2**20),
+        compiler_params=params,
     )(message)
     reply = lax.all_to_all(
         reply.reshape(LANES, 1, LANES), ACROSS, split_axis=0, concat_axis=0, tiled=True
@@ -187,12 +231,17 @@
     sketch, gram = pl.pallas_call(
         finish_kernel,
         name="finish",
-        out_shape=(jax.ShapeDtypeStruct((COLS, PICKS), f32), jax.ShapeDtypeStruct((1, LANES), f32)),
-        in_specs=[VMEM] * 3,
-        out_specs=(VMEM, VMEM),
-        compiler_params=pltpu.CompilerParams(vmem_limit_bytes=32 * 2**20),
-    )(reply, offsets, rank)
-    return sketch, gram[:, : COLS * COLS].reshape(COLS * COLS, 1)
+        out_shape=(jax.ShapeDtypeStruct((COLS, PICKS), f32), jax.ShapeDtypeStruct((1, COLS * COLS), f32)),
+        in_specs=[VMEM] * 2,
+        out_specs=(HBM, HBM),
+        scratch_shapes=[
+            pltpu.VMEM((COLS, PICKS), f32),
+            pltpu.VMEM((1, COLS * COLS), f32),
+            pltpu.SemaphoreType.DMA((2,)),
+        ],
+        compiler_params=params,
+    )(reply, slots)
+    return sketch, gram.reshape(COLS * COLS, 1)
 
 
 def solution(mesh):

time: 46.5 us -> 43.6 us (0.938)
  local copies, waits for them, and re-layouts: 3.76 us -> 0 us
  Pallas kernels: 2.53 us -> 3.52 us
    unnamed x8 -> x0, local copies, waits for them, and re-layouts: 3.25 us -> none
    pallas_call x1, Pallas kernels: 0.65 us -> 1.62 us  [on_device(): pl.pallas_call(send_kernel, name='transform_sections', out_shape=(jax.Sha...]
    reshape x1 -> x0, local copies, waits for them, and re-layouts: 0.51 us -> none  [on_device(): return (sketch, gram[:, :COLS * COLS].reshape(COLS * COLS, 1))]
where the time goes in v2:
time: 43.6 us; the launch traced here: 43.5 us
  blocking collectives  39.3 us (90%)
  Pallas kernels  3.52 us (8%)
  between operations  0.64 us (1%)
    all_to_all x1, blocking collectives, on_device(): lax.all_to_all(message.reshape(LANES, 1, CHUNK * LANES), ACROSS, split_ax...  26.1 us
    all_to_all x1, blocking collectives, on_device(): lax.all_to_all(reply.reshape(LANES, 1, LANES), ACROSS, split_axis=0, conc...  13.2 us
    pallas_call x1, Pallas kernels, on_device(): pl.pallas_call(send_kernel, name='transform_sections', out_shape=(jax.Sha...  1.62 us
    pallas_call x1, Pallas kernels, on_device(): pl.pallas_call(finish_kernel, name='finish', out_shape=(jax.ShapeDtypeStr...  0.96 us
    pallas_call x1, Pallas kernels, on_device(): pl.pallas_call(answer_kernel, name='answer', out_shape=jax.ShapeDtypeStru...  0.94 us

profile of v2, /device:TPU:1, one launch (start us, length us, event | category | flops | bytes accessed | tf_op | source)
XLA Modules:
  0.0 43.5 jit_solution(2057957035660211213)
XLA Ops:
  0.6 1.6 %transform_sections.1 = (f32[1152,128]{1,0:T(8,128)S(1)}, s32[1,1024]{1,0:T(1,128)S(1)}) custom-call(f32[8,16384]{1,0:T(8,128)} %matrix_hbm.1, s32[128,128]{1,0:T(8,128)} %bitcast.14, s32[1,1024]{1,0:T(1,128)} %bitcast.15, s32[1,1024]{1,0:T(1,128)} %bitcast.16), custom_call_target="tpu_custom_call" | custom-call | tf_op jit(solution)/shard_map/transform_sections/pallas_call | solution.py:183
  2.3 26.1 %all_to_all.10 = f32[128,1,1152]{2,1,0:T(1,128)S(1)} all-to-all(f32[128,1,1152]{2,1,0:T(1,128)S(1)} %bitcast.11), channel_id=1, replica_groups=mesh['wide'=32,'narrow'=4] {'wide','narrow'}, dimensions={0} | all-to-all | bytes 1179648 | tf_op jit(solution)/shard_map/all_to_all | solution.py:212
  28.4 0.9 %answer.1 = f32[128,128]{1,0:T(8,128)S(1)} custom-call(f32[1152,128]{1,0:T(8,128)S(1)} %bitcast.10), custom_call_target="tpu_custom_call" | custom-call | tf_op jit(solution)/shard_map/answer/pallas_call | solution.py:215
  29.3 13.2 %all_to_all.11 = f32[128,1,128]{2,1,0:T(1,128)S(1)} all-to-all(f32[128,1,128]{2,1,0:T(1,128)S(1)} %bitcast.12), channel_id=1, replica_groups=mesh['wide'=32,'narrow'=4] {'wide','narrow'}, dimensions={0} | all-to-all | bytes 131072 | tf_op jit(solution)/shard_map/all_to_all | solution.py:228
  42.5 1.0 %finish.1 = (f32[8,1024]{1,0:T(8,128)}, f32[1,64]{1,0:T(1,128)}) custom-call(f32[128,128]{1,0:T(8,128)S(1)} %bitcast.13, s32[1,1024]{1,0:T(1,128)S(1)} %get-tuple-element.7.slots), custom_call_target="tpu_custom_call" | custom-call | tf_op jit(solution)/shard_map/finish/pallas_call | solution.py:231

commit v3 on v2

v3 whole, which is shorter than its diff:
```python
import math

import jax
import jax.numpy as jnp
from jax import lax
from jax.experimental import pallas as pl
from jax.experimental.pallas import tpu as pltpu
from jax.sharding import Mesh
from jax.sharding import PartitionSpec as P

LANES = 128
CHIPS = 64
HALVES = 2
SLOTS = 8
COLS = 8
CHUNK = HALVES * COLS + 1
PICKS = LANES * SLOTS
PIECES = 4
FIRST = 42
VMEM = pl.BlockSpec(memory_space=pltpu.VMEM)
HBM = pl.BlockSpec(memory_space=pltpu.HBM)


def device(chip, core):
    return (chip >> 2) * 8 + core * 4 + (chip & 3)


def exchange(rows):
    groups = [[device(j ^ FIRST, core) for j in range(CHIPS)] for core in range(2)]
    parts = rows.reshape(CHIPS, 1, -1)
    parts = lax.all_to_all(parts, "all", split_axis=0, concat_axis=0, tiled=True, axis_index_groups=groups)
    return parts.reshape(rows.shape)


def other_core(value):
    return lax.ppermute(value, "all", [(i, i ^ 4) for i in range(2 * CHIPS)])


def walsh(tiles):
    span = 1
    while span < len(tiles):
        out = list(tiles)
        for i in range(len(tiles)):
            if not i & span:
                out[i] = tiles[i] + tiles[i | span]
                out[i | span] = tiles[i] - tiles[i | span]
        tiles = out
        span *= 2
    return tiles


def one_hot(index, count):
    rows = lax.broadcasted_iota(jnp.int32, (count, index.shape[1]), 0)
    return (rows == index).astype(jnp.float32)


def split(values):
    high = values.astype(jnp.bfloat16)
    return high, (values - high.astype(jnp.float32)).astype(jnp.bfloat16)


def requests(place, owner):
    section = lax.shift_right_logical(place, 7)
    part = lax.shift_right_logical(section, 1) ^ FIRST
    hot = one_hot((section & 1) * CHIPS + part, LANES)
    before = lax.broadcasted_iota(jnp.int32, (LANES, LANES), 0) < lax.broadcasted_iota(jnp.int32, (LANES, LANES), 1)
    table = jnp.concatenate([before.astype(jnp.float32), jnp.ones((LANES, LANES), jnp.float32)], axis=1)
    table = table.astype(jnp.bfloat16)
    carry = jnp.zeros((LANES, LANES), jnp.float32)
    ranks = []
    for t in range(SLOTS):
        some = hot[:, t * LANES : (t + 1) * LANES]
        sums = jnp.dot(some.astype(jnp.bfloat16), table, preferred_element_type=jnp.float32)
        ranks.append(jnp.sum(some * (sums[:, :LANES] + carry), axis=0, keepdims=True))
        carry = carry + sums[:, LANES:]
    rank = jnp.concatenate(ranks, axis=1).astype(jnp.int32)
    slot = lax.broadcasted_iota(jnp.int32, (SLOTS, PICKS), 0) == rank
    low = (place & (LANES - 1)).astype(jnp.float32)
    wanted = jnp.concatenate(
        [jnp.where(slot, owner.astype(jnp.float32), 0.0), jnp.where(slot, low, 0.0)], axis=0
    )
    found = lax.dot_general(
        hot.astype(jnp.bfloat16),
        wanted.astype(jnp.bfloat16),
        (((1,), (1,)), ((), ())),
        preferred_element_type=jnp.float32,
    )
    row = lax.broadcasted_iota(jnp.int32, (LANES, SLOTS), 0)
    section_of = (((row & (CHIPS - 1)) ^ FIRST) * 2 + lax.shift_right_logical(row, 6)).astype(jnp.float32)
    rows = found[:, :SLOTS] * float(LANES * LANES) + section_of * float(LANES) + found[:, SLOTS:]
    return rank, jnp.concatenate([rows[:CHIPS], rows[CHIPS:]], axis=1)


def send_kernel(
    matrix_hbm, flips_hbm, owners_hbm, offsets_hbm, message, own, slots, matrix, flips, owners, offsets, mid, arrived
):
    copies = [
        pltpu.make_async_copy(source, target, arrived.at[i])
        for i, (source, target) in enumerate(
            ((offsets_hbm, offsets), (owners_hbm, owners), (flips_hbm, flips))
        )
    ]
    width = matrix.shape[1] // PIECES
    for p in range(PIECES):
        cut = pl.ds(p * width, width)
        copies.append(pltpu.make_async_copy(matrix_hbm.at[:, cut], matrix.at[:, cut], arrived.at[3 + p]))
    for copy in copies:
        copy.start()

    copies[0].wait()
    copies[1].wait()
    place = offsets[...]
    rank, rows = requests(place, owners[...])
    own[...] = jnp.concatenate([rows, jnp.zeros((CHIPS, LANES - HALVES * SLOTS), jnp.float32)], axis=1)
    section = lax.shift_right_logical(place, 7)
    part = lax.shift_right_logical(section, 1) ^ FIRST
    slots[...] = part * (HALVES * SLOTS) + (section & 1) * SLOTS + rank

    scale = 1.0 / math.sqrt(float(LANES) ** 3)
    copies[2].wait()
    signs = jnp.where(flips[...] == 1, scale, -scale)
    for i in range(16):
        if i * PIECES % 16 == 0:
            copies[3 + i * PIECES // 16].wait()
        tiles = []
        for f in range(i * 8, i * 8 + 8):
            tiles.append(matrix[:, f * LANES : (f + 1) * LANES] * signs[f : f + 1, :])
        for j, tile in enumerate(walsh(tiles)):
            mid[i * 8 + j] = tile
    for j in range(8):
        for i, tile in enumerate(walsh([mid[i * 8 + j] for i in range(16)])):
            section = i * 8 + j
            row = ((section >> 1) ^ FIRST) * CHUNK + (section & 1) * COLS
            message[pl.ds(row, COLS), :] = tile


def ask_kernel(_, own, owners, offsets, message):
    _, rows = requests(offsets[...], owners[...])
    count = HALVES * SLOTS
    rows = jnp.concatenate(
        [jnp.zeros((CHIPS, count), jnp.float32), rows, jnp.zeros((CHIPS, LANES - 2 * count), jnp.float32)], axis=1
    )
    message[pl.ds(CHUNK - 1, CHIPS, stride=CHUNK), :] = own[...] + rows


def bit_sign(index, bit):
    return 1.0 - 2.0 * (lax.shift_right_logical(index, bit) & 1).astype(jnp.float32)


def sign_table(index, bits):
    row = lax.broadcasted_iota(jnp.int32, (8, index.shape[1]), 0)
    block = jnp.ones((8, index.shape[1]), jnp.float32)
    for b in range(3):
        block = block * jnp.where(lax.shift_right_logical(row, b) & 1 == 1, bit_sign(index, b), 1.0)
    blocks = [block]
    for b in range(3, bits):
        factor = bit_sign(index, b)
        blocks = blocks + [block * factor for block in blocks]
    return jnp.concatenate(blocks, axis=0)


def answer_kernel(message, reply, left, right, signs):
    core = lax.shift_right_logical(lax.axis_index("all"), 2) & 1
    wanted = message[pl.ds(CHUNK - 1, CHIPS, stride=CHUNK), :]
    wanted = jnp.concatenate([wanted, pltpu.roll(wanted, LANES - HALVES * SLOTS, 1)], axis=0)
    wanted = wanted.T[: HALVES * SLOTS, :].astype(jnp.int32)
    factors = []
    for n in range(HALVES * SLOTS):
        index = wanted[n : n + 1, :]
        cut = slice(n * LANES, (n + 1) * LANES)
        table = sign_table(index & (LANES - 1), 7).astype(jnp.bfloat16)
        right[:LANES, cut] = table
        right[LANES:, cut] = table
        owner = lax.shift_right_logical(index, 14)
        chip = lax.shift_right_logical(owner, 3) * 4 + (owner & 3)
        signs[:, cut] = sign_table(chip, 6)
        factor = bit_sign(owner & (core * 4), 2)
        for b in range(6):
            if FIRST >> b & 1:
                factor = factor * bit_sign(chip, b)
        factors.append(factor)
    for half in range(HALVES):
        for pair in range(CHIPS // 2):
            tile = jnp.concatenate(
                [message[pl.ds(j * CHUNK + half * COLS, COLS), :] for j in (2 * pair, 2 * pair + 1)], axis=0
            )
            high, low = split(tile)
            left[half, pl.ds(pair * 16, 16), :LANES] = high
            left[half, pl.ds(pair * 16, 16), LANES:] = low
    answers = []
    width = 256
    for half in range(HALVES):
        for n in range(PICKS // width):
            cut = slice(half * PICKS + n * width, half * PICKS + (n + 1) * width)
            total = jnp.zeros((COLS, width), jnp.float32)
            for m in range(2):
                part = jnp.dot(
                    left[half, m * 256 : (m + 1) * 256, :], right[:, cut], preferred_element_type=jnp.float32
                )
                for j in range(32):
                    total = total + part[j * COLS : (j + 1) * COLS, :] * signs[m * 32 + j : m * 32 + j + 1, cut]
            answers += [total[:, :LANES], total[:, LANES:]]
    answers = [answer * factor for answer, factor in zip(answers, factors)]
    answers = jnp.concatenate(answers, axis=0).T
    for t in range(2):
        reply[pl.ds(t, CHIPS, stride=2), :] = answers[t * CHIPS : (t + 1) * CHIPS, :]


def finish_kernel(reply, other, slots, sketch_hbm, gram_hbm, sketch, gram, sent):
    count = HALVES * SLOTS
    place = slots[...]
    hot = one_hot(lax.shift_right_logical(place, 4), CHIPS).astype(jnp.bfloat16)
    answers = jnp.concatenate(
        [reply[pl.ds(0, CHIPS, stride=2), :], other[pl.ds(1, CHIPS, stride=2), :]], axis=0
    )
    parts = jnp.dot(
        jnp.concatenate(split(answers.T), axis=1),
        jnp.concatenate([hot] * 4, axis=0),
        preferred_element_type=jnp.float32,
    )
    place = place & (count - 1)
    total = jnp.zeros((COLS, PICKS), jnp.float32)
    for n in range(count):
        total = total + jnp.where(place == n, parts[n * COLS : (n + 1) * COLS, :], 0.0)
    sketch[...] = total
    first = pltpu.make_async_copy(sketch, sketch_hbm, sent.at[0])
    first.start()
    products = []
    for a in range(COLS):
        product = total * total[a : a + 1, :]
        products.append(sum(product[:, t * LANES : (t + 1) * LANES] for t in range(SLOTS)))
    products = jnp.concatenate(products + [jnp.zeros((LANES - COLS * COLS, LANES), jnp.float32)], axis=0)
    products = jnp.sum(products.T, axis=0, keepdims=True) * (1.0 / PICKS)
    gram[...] = products[:, : COLS * COLS]
    second = pltpu.make_async_copy(gram, gram_hbm, sent.at[1])
    second.start()
    first.wait()
    second.wait()


def on_device(matrix, flips, owners, offsets):
    f32, i32 = jnp.float32, jnp.int32
    params = pltpu.CompilerParams(vmem_limit_bytes=32 * 2**20)
    owners = owners.reshape(1, PICKS)
    offsets = offsets.reshape(1, PICKS)
    owners_other = other_core(owners)
    offsets_other = other_core(offsets)
    message_shape = jax.ShapeDtypeStruct((CHIPS * CHUNK, LANES), f32)
    message, own, slots = pl.pallas_call(
        send_kernel,
        name="transform_sections",
        out_shape=(
            message_shape,
            jax.ShapeDtypeStruct((CHIPS, LANES), f32),
            jax.ShapeDtypeStruct((1, PICKS), i32),
        ),
        in_specs=[HBM] * 4,
        out_specs=(VMEM, VMEM, VMEM),
        scratch_shapes=[
            pltpu.VMEM((COLS, LANES * LANES), f32),
            pltpu.VMEM((LANES, LANES), i32),
            pltpu.VMEM((1, PICKS), i32),
            pltpu.VMEM((1, PICKS), i32),
            pltpu.VMEM((LANES, COLS, LANES), f32),
            pltpu.SemaphoreType.DMA((3 + PIECES,)),
        ],
        compiler_params=params,
        cost_estimate=pl.CostEstimate(flops=2**22, bytes_accessed=4 * 2**20, transcendentals=0),
    )(
        *(
            pltpu.with_memory_space_constraint(operand, pltpu.HBM)
            for operand in (matrix, flips.reshape(LANES, LANES), owners, offsets)
        )
    )
    message = pl.pallas_call(
        ask_kernel,
        name="other_requests",
        out_shape=message_shape,
        in_specs=[VMEM] * 4,
        out_specs=VMEM,
        input_output_aliases={0: 0},
        compiler_params=params,
    )(message, own, owners_other, offsets_other)
    message = exchange(message)
    reply = pl.pallas_call(
        answer_kernel,
        name="answer",
        out_shape=jax.ShapeDtypeStruct((LANES, LANES), f32),
        in_specs=[VMEM],
        out_specs=VMEM,
        scratch_shapes=[
            pltpu.VMEM((HALVES, CHIPS * COLS, 2 * LANES), jnp.bfloat16),
            pltpu.VMEM((2 * LANES, HALVES * PICKS), jnp.bfloat16),
            pltpu.VMEM((CHIPS, HALVES * PICKS), f32),
        ],
        compiler_params=params,
    )(message)
    reply = exchange(reply)
    sketch, gram = pl.pallas_call(
        finish_kernel,
        name="finish",
        out_shape=(jax.ShapeDtypeStruct((COLS, PICKS), f32), jax.ShapeDtypeStruct((1, COLS * COLS), f32)),
        in_specs=[VMEM] * 3,
        out_specs=(HBM, HBM),
        scratch_shapes=[
            pltpu.VMEM((COLS, PICKS), f32),
            pltpu.VMEM((1, COLS * COLS), f32),
            pltpu.SemaphoreType.DMA((2,)),
        ],
        compiler_params=params,
    )(reply, other_core(reply), slots)
    return sketch, gram.reshape(COLS * COLS, 1)


def solution(mesh):
    flat = Mesh(mesh.devices.reshape(-1), ("all",))
    in_specs = (P(None, "all"), P("all"), P("all", None), P("all"))
    out_specs = (P(None, "all"), P(None, "all"))
    return jax.shard_map(on_device, mesh=flat, in_specs=in_specs, out_specs=out_specs, check_vma=False)
```

time: 43.6 us -> 42.4 us (0.972)
  blocking collectives: 39.3 us -> 31.9 us
  starting transfers between devices: 0 us -> 4.49 us
  waiting for transfers between devices: 0 us -> 0.91 us
  Pallas kernels: 3.52 us -> 4.27 us
    all_to_all x2, blocking collectives: 39.3 us -> 31.9 us  [exchange(): lax.all_to_all(parts, 'all', split_axis=0, concat_axis=0, tiled=True, axi...]
    ppermute x0 -> x3, starting transfers between devices: none -> 4.49 us  [other_core(): return lax.ppermute(value, 'all', [(i, i ^ 4) for i in range(2 * CHIPS)])]
    ppermute x0 -> x3, waiting for transfers between devices: none -> 0.91 us  [other_core(): return lax.ppermute(value, 'all', [(i, i ^ 4) for i in range(2 * CHIPS)])]
    pallas_call x1 -> x2, Pallas kernels: 1.62 us -> 2.3 us  [the longest x1 1.59 us: on_device(): pl.pallas_call(send_kernel, name='transform_sections', out_shape=(message...]
  transfers between devices with their start and end apart: 0 -> 3, of which waited for: 0 -> 1; matrix products, arithmetic and copies ran while one was open for 0% -> 0% of each run, Pallas kernels for 0% -> 4%
where the time goes in v3:
time: 42.4 us; the launch traced here: 42.2 us
  blocking collectives  31.9 us (75%)
  starting transfers between devices  4.49 us (11%)
  Pallas kernels  4.27 us (10%)
  waiting for transfers between devices  0.91 us (2%)
  between operations  0.66 us (2%)
    all_to_all x2, blocking collectives, exchange(): lax.all_to_all(parts, 'all', split_axis=0, concat_axis=0, tiled=True, axi...  31.9 us
    ppermute x3, starting transfers between devices, other_core(): return lax.ppermute(value, 'all', [(i, i ^ 4) for i in range(2 * CHIPS)])  4.49 us
    pallas_call x1, Pallas kernels, on_device(): pl.pallas_call(send_kernel, name='transform_sections', out_shape=(message...  1.59 us
    pallas_call x1, Pallas kernels, on_device(): pl.pallas_call(answer_kernel, name='answer', out_shape=jax.ShapeDtypeStru...  1.04 us
    pallas_call x1, Pallas kernels, on_device(): pl.pallas_call(finish_kernel, name='finish', out_shape=(jax.ShapeDtypeStr...  0.92 us
    ppermute x3, waiting for transfers between devices, other_core(): return lax.ppermute(value, 'all', [(i, i ^ 4) for i in range(2 * CHIPS)])  0.91 us
  transfers between devices with their start and end apart: 3, of which 1 were waited for; matrix products, arithmetic and copies ran while one was open for 0% of the time, Pallas kernels for 4%

profile of v3, /device:TPU:1, one launch (start us, length us, event | category | flops | bytes accessed | tf_op | source)
XLA Modules:
  0.0 42.2 jit_solution(13915998840638042978)
XLA Ops:
  0.6 1.5 %collective-permute-start = (s32[1,1024]{1,0:T(1,128)}, s32[1,1024]{1,0:T(1,128)S(1)}, u32[]{:S(2)}, u32[]{:S(2)}) collective-permute-start(s32[1,1024]{1,0:T(1,128)} %bitcast.14), channel_id=1, source_target_pairs={{0,4},{1,5},{2,6},{3,7},{4,0},{5,1},{6,2},{7,3},{8,12},{9,13},{10,... | collective-permute-start | bytes 12296 | tf_op jit(solution)/shard_map/ppermute | solution.py:36
  2.1 0.1 collective-permute-start.1
  2.2 1.6 %transform_sections.1 = (f32[1088,128]{1,0:T(8,128)S(1)}, f32[64,128]{1,0:T(8,128)S(1)}, s32[1,1024]{1,0:T(1,128)S(1)}) custom-call(f32[8,16384]{1,0:T(8,128)} %matrix_hbm.1, s32[128,128]{1,0:T(8,128)} %bitcast.13, s32[1,1024]{1,0:T(1,128)} %bitcast.15, s32[1,1024]{1,0:T(1,128)} %bitcast.17), custom_call_target="tpu_custom_call" | custom-call | flops 4194304 | bytes 4194304 | tf_op jit(solution)/shard_map/transform_sections/pallas_call | solution.py:249
  3.8 0.0 collective-permute-done.owners
  3.8 0.0 collective-permute-done.1.offsets
  3.8 0.7 %other_requests.1 = f32[1088,128]{1,0:T(8,128)S(1)} custom-call(f32[1088,128]{1,0:T(8,128)S(1)} %get-tuple-element.7._, f32[64,128]{1,0:T(8,128)S(1)} %get-tuple-element.8.own, s32[1,1024]{1,0:T(1,128)S(1)} %collective-permute-done.owners, s32[1,1024]{1,0:T(1,128)S(1)} %collective-permute-done.1.offsets), custom_call_target="tpu_custom_call", output_to_operand_aliasing={{}: (0, {})} | custom-call | tf_op jit(solution)/shard_map/other_requests/pallas_call | solution.py:275
  4.6 19.7 %all_to_all.10 = f32[64,1,2176]{2,1,0:T(1,128)S(1)} all-to-all(f32[64,1,2176]{2,1,0:T(1,128)S(1)} %bitcast.8), channel_id=1, replica_groups={{82,83,80,81,90,91,88,89,66,67,64,65,74,75,72,73,114,115,112,113,122,12..., dimensions={0} | all-to-all | bytes 1114112 | tf_op jit(solution)/shard_map/all_to_all | solution.py:31
  24.3 1.0 %answer.1 = f32[128,128]{1,0:T(8,128)S(1)} custom-call(f32[1088,128]{1,0:T(8,128)S(1)} %bitcast.9), custom_call_target="tpu_custom_call" | custom-call | tf_op jit(solution)/shard_map/answer/pallas_call | solution.py:285
  25.3 12.2 %all_to_all.11 = f32[64,1,256]{2,1,0:T(1,128)S(1)} all-to-all(f32[64,1,256]{2,1,0:T(1,128)S(1)} %bitcast.10), channel_id=1, replica_groups={{82,83,80,81,90,91,88,89,66,67,64,65,74,75,72,73,114,115,112,113,122,12..., dimensions={0} | all-to-all | bytes 131072 | tf_op jit(solution)/shard_map/all_to_all | solution.py:31
  37.5 2.9 %collective-permute-start.2 = (f32[128,128]{1,0:T(8,128)S(1)}, f32[128,128]{1,0:T(8,128)S(1)}, u32[]{:S(2)}, u32[]{:S(2)}) collective-permute-start(f32[128,128]{1,0:T(8,128)S(1)} %bitcast.11), channel_id=1, source_target_pairs={{0,4},{1,5},{2,6},{3,7},{4,0},{5,1},{6,2},{7,3},{8,12},{9,13},{10,... | collective-permute-start | bytes 196616 | tf_op jit(solution)/shard_map/ppermute | solution.py:36
  40.4 0.9 %collective-permute-done.2.other = f32[128,128]{1,0:T(8,128)S(1)} collective-permute-done((f32[128,128]{1,0:T(8,128)S(1)}, f32[128,128]{1,0:T(8,128)S(1)}, u32[]{:S(2)}, u32[]{:S(2)}) %collective-permute-start.2) | collective-permute-done | bytes 65568 | tf_op jit(solution)/shard_map/ppermute | solution.py:36
  41.3 0.9 %finish.1 = (f32[8,1024]{1,0:T(8,128)}, f32[1,64]{1,0:T(1,128)}) custom-call(f32[128,128]{1,0:T(8,128)S(1)} %bitcast.12, f32[128,128]{1,0:T(8,128)S(1)} %collective-permute-done.2.other, s32[1,1024]{1,0:T(1,128)S(1)} %get-tuple-element.9.slots), custom_call_target="tpu_custom_call" | custom-call | tf_op jit(solution)/shard_map/finish/pallas_call | solution.py:299
Async XLA Ops:
  0.6 3.2 %collective-permute-start = (s32[1,1024]{1,0:T(1,128)}, s32[1,1024]{1,0:T(1,128)S(1)}, u32[]{:S(2)}, u32[]{:S(2)}) collective-permute-start(s32[1,1024]{1,0:T(1,128)} %bitcast.14), channel_id=1, source_target_pairs={{0,4},{1,5},{2,6},{3,7},{4,0},{5,1},{6,2},{7,3},{8,12},{9,13},{10,... | collective-permute-start | bytes 12296 | tf_op jit(solution)/shard_map/ppermute | solution.py:36
  2.1 1.7 %collective-permute-start.1 = (s32[1,1024]{1,0:T(1,128)}, s32[1,1024]{1,0:T(1,128)S(1)}, u32[]{:S(2)}, u32[]{:S(2)}) collective-permute-start(s32[1,1024]{1,0:T(1,128)} %bitcast.16), channel_id=1, source_target_pairs={{0,4},{1,5},{2,6},{3,7},{4,0},{5,1},{6,2},{7,3},{8,12},{9,13},{10,... | collective-permute-start | bytes 12296 | tf_op jit(solution)/shard_map/ppermute | solution.py:36
  37.5 3.8 %collective-permute-start.2 = (f32[128,128]{1,0:T(8,128)S(1)}, f32[128,128]{1,0:T(8,128)S(1)}, u32[]{:S(2)}, u32[]{:S(2)}) collective-permute-start(f32[128,128]{1,0:T(8,128)S(1)} %bitcast.11), channel_id=1, source_target_pairs={{0,4},{1,5},{2,6},{3,7},{4,0},{5,1},{6,2},{7,3},{8,12},{9,13},{10,... | collective-permute-start | bytes 196616 | tf_op jit(solution)/shard_map/ppermute | solution.py:36

commit v4 on v3

--- a/solution.py
+++ b/solution.py
@@ -159,7 +159,7 @@
     return jnp.concatenate(blocks, axis=0)
 
 
-def answer_kernel(message, reply, left, right, signs):
+def answer_kernel(message, mine, theirs, left, right, signs):
     core = lax.shift_right_logical(lax.axis_index("all"), 2) & 1
     wanted = message[pl.ds(CHUNK - 1, CHIPS, stride=CHUNK), :]
     wanted = jnp.concatenate([wanted, pltpu.roll(wanted, LANES - HALVES * SLOTS, 1)], axis=0)
@@ -202,21 +202,17 @@
             answers += [total[:, :LANES], total[:, LANES:]]
     answers = [answer * factor for answer, factor in zip(answers, factors)]
     answers = jnp.concatenate(answers, axis=0).T
-    for t in range(2):
-        reply[pl.ds(t, CHIPS, stride=2), :] = answers[t * CHIPS : (t + 1) * CHIPS, :]
-
-
-def finish_kernel(reply, other, slots, sketch_hbm, gram_hbm, sketch, gram, sent):
+    mine[...] = answers[:CHIPS, :]
+    theirs[...] = answers[CHIPS:, :]
+
+
+def finish_kernel(reply, slots, sketch_hbm, gram_hbm, sketch, gram, sent):
     count = HALVES * SLOTS
     place = slots[...]
     hot = one_hot(lax.shift_right_logical(place, 4), CHIPS).astype(jnp.bfloat16)
-    answers = jnp.concatenate(
-        [reply[pl.ds(0, CHIPS, stride=2), :], other[pl.ds(1, CHIPS, stride=2), :]], axis=0
-    )
+    answers = jnp.concatenate([part.astype(jnp.float32) for part in split(reply[...])], axis=0)
     parts = jnp.dot(
-        jnp.concatenate(split(answers.T), axis=1),
-        jnp.concatenate([hot] * 4, axis=0),
-        preferred_element_type=jnp.float32,
+        answers.T.astype(jnp.bfloat16), jnp.concatenate([hot, hot], axis=0), preferred_element_type=jnp.float32
     )
     place = place & (count - 1)
     total = jnp.zeros((COLS, PICKS), jnp.float32)
@@ -282,12 +278,13 @@
         compiler_params=params,
     )(message, own, owners_other, offsets_other)
     message = exchange(message)
-    reply = pl.pallas_call(
+    half_shape = jax.ShapeDtypeStruct((CHIPS, LANES), f32)
+    mine, theirs = pl.pallas_call(
         answer_kernel,
         name="answer",
-        out_shape=jax.ShapeDtypeStruct((LANES, LANES), f32),
+        out_shape=(half_shape, half_shape),
         in_specs=[VMEM],
-        out_specs=VMEM,
+        out_specs=(VMEM, VMEM),
         scratch_shapes=[
             pltpu.VMEM((HALVES, CHIPS * COLS, 2 * LANES), jnp.bfloat16),
             pltpu.VMEM((2 * LANES, HALVES * PICKS), jnp.bfloat16),
@@ -295,12 +292,12 @@
         ],
         compiler_params=params,
     )(message)
-    reply = exchange(reply)
+    reply = exchange(mine + other_core(theirs))
     sketch, gram = pl.pallas_call(
         finish_kernel,
         name="finish",
         out_shape=(jax.ShapeDtypeStruct((COLS, PICKS), f32), jax.ShapeDtypeStruct((1, COLS * COLS), f32)),
-        in_specs=[VMEM] * 3,
+        in_specs=[VMEM] * 2,
         out_specs=(HBM, HBM),
         scratch_shapes=[
             pltpu.VMEM((COLS, PICKS), f32),
@@ -308,7 +305,7 @@
             pltpu.SemaphoreType.DMA((2,)),
         ],
         compiler_params=params,
-    )(reply, other_core(reply), slots)
+    )(reply, slots)
     return sketch, gram.reshape(COLS * COLS, 1)
 
 

time: 42.4 us -> 41.2 us (0.972)
  starting transfers between devices: 4.49 us -> 2.85 us
    ppermute x3, starting transfers between devices: 4.49 us -> 2.85 us  [other_core(): return lax.ppermute(value, 'all', [(i, i ^ 4) for i in range(2 * CHIPS)])]
where the time goes in v4:
time: 41.2 us; the launch traced here: 40.7 us
  blocking collectives  32 us (78%)
  Pallas kernels  4.27 us (10%)
  starting transfers between devices  2.85 us (7%)
  waiting for transfers between devices  0.87 us (2%)
  between operations  0.67 us (2%)
    all_to_all x2, blocking collectives, exchange(): lax.all_to_all(parts, 'all', split_axis=0, concat_axis=0, tiled=True, axi...  32 us
    ppermute x3, starting transfers between devices, other_core(): return lax.ppermute(value, 'all', [(i, i ^ 4) for i in range(2 * CHIPS)])  2.85 us
    pallas_call x1, Pallas kernels, on_device(): pl.pallas_call(send_kernel, name='transform_sections', out_shape=(message...  1.59 us
    pallas_call x1, Pallas kernels, on_device(): pl.pallas_call(answer_kernel, name='answer', out_shape=(half_shape, half_...  1.04 us
    pallas_call x1, Pallas kernels, on_device(): pl.pallas_call(finish_kernel, name='finish', out_shape=(jax.ShapeDtypeStr...  0.93 us
    ppermute x3, waiting for transfers between devices, other_core(): return lax.ppermute(value, 'all', [(i, i ^ 4) for i in range(2 * CHIPS)])  0.87 us
  transfers between devices with their start and end apart: 3, of which 1 were waited for; matrix products, arithmetic and copies ran while one was open for 0% of the time, Pallas kernels for 4%

profile of v4, /device:TPU:1, one launch (start us, length us, event | category | flops | bytes accessed | tf_op | source)
XLA Modules:
  0.0 40.7 jit_solution(15618793284733855711)
XLA Ops:
  0.6 1.5 %collective-permute-start = (s32[1,1024]{1,0:T(1,128)}, s32[1,1024]{1,0:T(1,128)S(1)}, u32[]{:S(2)}, u32[]{:S(2)}) collective-permute-start(s32[1,1024]{1,0:T(1,128)} %bitcast.15), channel_id=1, source_target_pairs={{0,4},{1,5},{2,6},{3,7},{4,0},{5,1},{6,2},{7,3},{8,12},{9,13},{10,... | collective-permute-start | bytes 12296 | tf_op jit(solution)/shard_map/ppermute | solution.py:36
  2.1 0.1 collective-permute-start.1
  2.2 1.6 %transform_sections.1 = (f32[1088,128]{1,0:T(8,128)S(1)}, f32[64,128]{1,0:T(8,128)S(1)}, s32[1,1024]{1,0:T(1,128)S(1)}) custom-call(f32[8,16384]{1,0:T(8,128)} %matrix_hbm.1, s32[128,128]{1,0:T(8,128)} %bitcast.14, s32[1,1024]{1,0:T(1,128)} %bitcast.16, s32[1,1024]{1,0:T(1,128)} %bitcast.18), custom_call_target="tpu_custom_call" | custom-call | flops 4194304 | bytes 4194304 | tf_op jit(solution)/shard_map/transform_sections/pallas_call | solution.py:245
  3.8 0.0 collective-permute-done.owners
  3.8 0.0 collective-permute-done.1.offsets
  3.8 0.7 %other_requests.1 = f32[1088,128]{1,0:T(8,128)S(1)} custom-call(f32[1088,128]{1,0:T(8,128)S(1)} %get-tuple-element.9._, f32[64,128]{1,0:T(8,128)S(1)} %get-tuple-element.10.own, s32[1,1024]{1,0:T(1,128)S(1)} %collective-permute-done.owners, s32[1,1024]{1,0:T(1,128)S(1)} %collective-permute-done.1.offsets), custom_call_target="tpu_custom_call", output_to_operand_aliasing={{}: (0, {})} | custom-call | tf_op jit(solution)/shard_map/other_requests/pallas_call | solution.py:271
  4.6 19.7 %all_to_all.10 = f32[64,1,2176]{2,1,0:T(1,128)S(1)} all-to-all(f32[64,1,2176]{2,1,0:T(1,128)S(1)} %bitcast.10), channel_id=1, replica_groups={{82,83,80,81,90,91,88,89,66,67,64,65,74,75,72,73,114,115,112,113,122,12..., dimensions={0} | all-to-all | bytes 1114112 | tf_op jit(solution)/shard_map/all_to_all | solution.py:31
  24.3 1.0 %answer.1 = (f32[64,128]{1,0:T(8,128)S(1)}, f32[64,128]{1,0:T(8,128)S(1)}) custom-call(f32[1088,128]{1,0:T(8,128)S(1)} %bitcast.11), custom_call_target="tpu_custom_call" | custom-call | tf_op jit(solution)/shard_map/answer/pallas_call | solution.py:282
  25.3 1.3 %collective-permute-start.2 = (f32[64,128]{1,0:T(8,128)S(1)}, f32[64,128]{1,0:T(8,128)S(1)}, u32[]{:S(2)}, u32[]{:S(2)}) collective-permute-start(f32[64,128]{1,0:T(8,128)S(1)} %get-tuple-element.12), channel_id=1, source_target_pairs={{0,4},{1,5},{2,6},{3,7},{4,0},{5,1},{6,2},{7,3},{8,12},{9,13},{10,... | collective-permute-start | bytes 98312 | tf_op jit(solution)/shard_map/ppermute | solution.py:36
  26.6 0.9 %collective-permute-done.2 = f32[64,128]{1,0:T(8,128)S(1)} collective-permute-done((f32[64,128]{1,0:T(8,128)S(1)}, f32[64,128]{1,0:T(8,128)S(1)}, u32[]{:S(2)}, u32[]{:S(2)}) %collective-permute-start.2) | collective-permute-done | bytes 32800 | tf_op jit(solution)/shard_map/ppermute | solution.py:36
  27.4 12.3 %all_to_all.11 = f32[64,1,128]{2,1,0:T(1,128)S(1)} all-to-all(f32[64,1,128]{2,1,0:T(1,128)S(1)} %bitcast.13), channel_id=1, replica_groups={{82,83,80,81,90,91,88,89,66,67,64,65,74,75,72,73,114,115,112,113,122,12..., dimensions={0} | all-to-all | bytes 65536 | tf_op jit(solution)/shard_map/all_to_all | solution.py:31
  39.8 0.9 %finish.1 = (f32[8,1024]{1,0:T(8,128)}, f32[1,64]{1,0:T(1,128)}) custom-call(f32[64,128]{1,0:T(8,128)S(1)} %bitcast.12, s32[1,1024]{1,0:T(1,128)S(1)} %get-tuple-element.13.slots), custom_call_target="tpu_custom_call" | custom-call | tf_op jit(solution)/shard_map/finish/pallas_call | solution.py:296
  (1 shorter events, 0.0 us)
Async XLA Ops:
  0.6 3.2 %collective-permute-start = (s32[1,1024]{1,0:T(1,128)}, s32[1,1024]{1,0:T(1,128)S(1)}, u32[]{:S(2)}, u32[]{:S(2)}) collective-permute-start(s32[1,1024]{1,0:T(1,128)} %bitcast.15), channel_id=1, source_target_pairs={{0,4},{1,5},{2,6},{3,7},{4,0},{5,1},{6,2},{7,3},{8,12},{9,13},{10,... | collective-permute-start | bytes 12296 | tf_op jit(solution)/shard_map/ppermute | solution.py:36
  2.1 1.7 %collective-permute-start.1 = (s32[1,1024]{1,0:T(1,128)}, s32[1,1024]{1,0:T(1,128)S(1)}, u32[]{:S(2)}, u32[]{:S(2)}) collective-permute-start(s32[1,1024]{1,0:T(1,128)} %bitcast.17), channel_id=1, source_target_pairs={{0,4},{1,5},{2,6},{3,7},{4,0},{5,1},{6,2},{7,3},{8,12},{9,13},{10,... | collective-permute-start | bytes 12296 | tf_op jit(solution)/shard_map/ppermute | solution.py:36
  25.3 2.1 %collective-permute-start.2 = (f32[64,128]{1,0:T(8,128)S(1)}, f32[64,128]{1,0:T(8,128)S(1)}, u32[]{:S(2)}, u32[]{:S(2)}) collective-permute-start(f32[64,128]{1,0:T(8,128)S(1)} %get-tuple-element.12), channel_id=1, source_target_pairs={{0,4},{1,5},{2,6},{3,7},{4,0},{5,1},{6,2},{7,3},{8,12},{9,13},{10,... | collective-permute-start | bytes 98312 | tf_op jit(solution)/shard_map/ppermute | solution.py:36

commit v5 on v4

--- a/solution.py
+++ b/solution.py
@@ -16,7 +16,7 @@
 CHUNK = HALVES * COLS + 1
 PICKS = LANES * SLOTS
 PIECES = 4
-FIRST = 42
+FIRST = 46
 VMEM = pl.BlockSpec(memory_space=pltpu.VMEM)
 HBM = pl.BlockSpec(memory_space=pltpu.HBM)
 
@@ -62,17 +62,20 @@
 def requests(place, owner):
     section = lax.shift_right_logical(place, 7)
     part = lax.shift_right_logical(section, 1) ^ FIRST
-    hot = one_hot((section & 1) * CHIPS + part, LANES)
-    before = lax.broadcasted_iota(jnp.int32, (LANES, LANES), 0) < lax.broadcasted_iota(jnp.int32, (LANES, LANES), 1)
-    table = jnp.concatenate([before.astype(jnp.float32), jnp.ones((LANES, LANES), jnp.float32)], axis=1)
-    table = table.astype(jnp.bfloat16)
-    carry = jnp.zeros((LANES, LANES), jnp.float32)
+    mask = lax.broadcasted_iota(jnp.int32, (LANES, PICKS), 0) == (section & 1) * CHIPS + part
+    hot = jnp.where(mask, 1.0, 0.0)
+    first = lax.broadcasted_iota(jnp.int32, (2 * LANES, LANES), 0)
+    second = lax.broadcasted_iota(jnp.int32, (2 * LANES, LANES), 1)
+    table = jnp.where((first < second) | (first >= LANES), 1.0, 0.0).astype(jnp.bfloat16)
+    earlier = jnp.zeros((LANES, LANES), jnp.float32)
     ranks = []
     for t in range(SLOTS):
-        some = hot[:, t * LANES : (t + 1) * LANES]
-        sums = jnp.dot(some.astype(jnp.bfloat16), table, preferred_element_type=jnp.float32)
-        ranks.append(jnp.sum(some * (sums[:, :LANES] + carry), axis=0, keepdims=True))
-        carry = carry + sums[:, LANES:]
+        cut = slice(t * LANES, (t + 1) * LANES)
+        some = hot[:, cut]
+        before = jnp.concatenate([some, earlier], axis=1).astype(jnp.bfloat16)
+        count = jnp.dot(before, table, preferred_element_type=jnp.float32)
+        ranks.append(jnp.sum(jnp.where(mask[:, cut], count, 0.0), axis=0, keepdims=True))
+        earlier = earlier + some
     rank = jnp.concatenate(ranks, axis=1).astype(jnp.int32)
     slot = lax.broadcasted_iota(jnp.int32, (SLOTS, PICKS), 0) == rank
     low = (place & (LANES - 1)).astype(jnp.float32)
@@ -80,24 +83,24 @@
         [jnp.where(slot, owner.astype(jnp.float32), 0.0), jnp.where(slot, low, 0.0)], axis=0
     )
     found = lax.dot_general(
+        wanted.astype(jnp.bfloat16),
         hot.astype(jnp.bfloat16),
-        wanted.astype(jnp.bfloat16),
         (((1,), (1,)), ((), ())),
         preferred_element_type=jnp.float32,
     )
-    row = lax.broadcasted_iota(jnp.int32, (LANES, SLOTS), 0)
-    section_of = (((row & (CHIPS - 1)) ^ FIRST) * 2 + lax.shift_right_logical(row, 6)).astype(jnp.float32)
-    rows = found[:, :SLOTS] * float(LANES * LANES) + section_of * float(LANES) + found[:, SLOTS:]
-    return rank, jnp.concatenate([rows[:CHIPS], rows[CHIPS:]], axis=1)
+    column = lax.broadcasted_iota(jnp.int32, (SLOTS, LANES), 1)
+    section_of = (((column & (CHIPS - 1)) ^ FIRST) * 2 + lax.shift_right_logical(column, 6)).astype(jnp.float32)
+    rows = found[:SLOTS] * float(LANES * LANES) + section_of * float(LANES) + found[SLOTS:]
+    return rank, jnp.concatenate([rows, pltpu.roll(rows, CHIPS, 1)], axis=0)
 
 
 def send_kernel(
-    matrix_hbm, flips_hbm, owners_hbm, offsets_hbm, message, own, slots, matrix, flips, owners, offsets, mid, arrived
+    matrix_hbm, flips_hbm, owners_hbm, offsets_hbm, message, owners, offsets, matrix, flips, mid, arrived
 ):
     copies = [
         pltpu.make_async_copy(source, target, arrived.at[i])
         for i, (source, target) in enumerate(
-            ((offsets_hbm, offsets), (owners_hbm, owners), (flips_hbm, flips))
+            ((flips_hbm, flips), (owners_hbm, owners), (offsets_hbm, offsets))
         )
     ]
     width = matrix.shape[1] // PIECES
@@ -106,18 +109,8 @@
         copies.append(pltpu.make_async_copy(matrix_hbm.at[:, cut], matrix.at[:, cut], arrived.at[3 + p]))
     for copy in copies:
         copy.start()
-
+    scale = 1.0 / math.sqrt(float(LANES) ** 3)
     copies[0].wait()
-    copies[1].wait()
-    place = offsets[...]
-    rank, rows = requests(place, owners[...])
-    own[...] = jnp.concatenate([rows, jnp.zeros((CHIPS, LANES - HALVES * SLOTS), jnp.float32)], axis=1)
-    section = lax.shift_right_logical(place, 7)
-    part = lax.shift_right_logical(section, 1) ^ FIRST
-    slots[...] = part * (HALVES * SLOTS) + (section & 1) * SLOTS + rank
-
-    scale = 1.0 / math.sqrt(float(LANES) ** 3)
-    copies[2].wait()
     signs = jnp.where(flips[...] == 1, scale, -scale)
     for i in range(16):
         if i * PIECES % 16 == 0:
@@ -132,15 +125,21 @@
             section = i * 8 + j
             row = ((section >> 1) ^ FIRST) * CHUNK + (section & 1) * COLS
             message[pl.ds(row, COLS), :] = tile
-
-
-def ask_kernel(_, own, owners, offsets, message):
-    _, rows = requests(offsets[...], owners[...])
-    count = HALVES * SLOTS
-    rows = jnp.concatenate(
-        [jnp.zeros((CHIPS, count), jnp.float32), rows, jnp.zeros((CHIPS, LANES - 2 * count), jnp.float32)], axis=1
-    )
-    message[pl.ds(CHUNK - 1, CHIPS, stride=CHUNK), :] = own[...] + rows
+    copies[1].wait()
+    copies[2].wait()
+
+
+def ask_kernel(_, owners, offsets, owners_other, offsets_other, message, slots):
+    place = offsets[...]
+    rank, rows = requests(place, owners[...])
+    _, rows_other = requests(offsets_other[...], owners_other[...])
+    rest = jnp.zeros((LANES - 2 * HALVES * SLOTS, LANES), jnp.float32)
+    rows = jnp.concatenate([rows, rows_other, rest], axis=0).T
+    message[pl.ds(CHUNK - 1, CHIPS, stride=CHUNK), :] = rows[:CHIPS]
+    section = lax.shift_right_logical(place, 7)
+    part = lax.shift_right_logical(section, 1) ^ FIRST
+    slot = (section & 1) * SLOTS + rank
+    slots[...] = part * (HALVES * SLOTS) + (slot & 1) * SLOTS + lax.shift_right_logical(slot, 1)
 
 
 def bit_sign(index, bit):
@@ -159,14 +158,16 @@
     return jnp.concatenate(blocks, axis=0)
 
 
-def answer_kernel(message, mine, theirs, left, right, signs):
+def answer(message, kind, left, reply, right, signs):
     core = lax.shift_right_logical(lax.axis_index("all"), 2) & 1
+    count = HALVES * SLOTS
     wanted = message[pl.ds(CHUNK - 1, CHIPS, stride=CHUNK), :]
-    wanted = jnp.concatenate([wanted, pltpu.roll(wanted, LANES - HALVES * SLOTS, 1)], axis=0)
-    wanted = wanted.T[: HALVES * SLOTS, :].astype(jnp.int32)
+    even, odd = [(LANES - kind * count - n) % LANES for n in range(2)]
+    wanted = jnp.concatenate([pltpu.roll(wanted, even, 1) if even else wanted, pltpu.roll(wanted, odd, 1)], axis=0)
+    wanted = wanted.T[:count, :].astype(jnp.int32)
     factors = []
-    for n in range(HALVES * SLOTS):
-        index = wanted[n : n + 1, :]
+    for n in range(count // 2):
+        index = wanted[2 * n : 2 * n + 1, :]
         cut = slice(n * LANES, (n + 1) * LANES)
         table = sign_table(index & (LANES - 1), 7).astype(jnp.bfloat16)
         right[:LANES, cut] = table
@@ -179,6 +180,24 @@
             if FIRST >> b & 1:
                 factor = factor * bit_sign(chip, b)
         factors.append(factor)
+    answers = []
+    width = 256
+    for half in range(HALVES):
+        for n in range(PICKS // 2 // width):
+            cut = slice(half * PICKS // 2 + n * width, half * PICKS // 2 + (n + 1) * width)
+            total = jnp.zeros((COLS, width), jnp.float32)
+            for m in range(2):
+                part = jnp.dot(
+                    left[half, m * 256 : (m + 1) * 256, :], right[:, cut], preferred_element_type=jnp.float32
+                )
+                for j in range(32):
+                    total = total + part[j * COLS : (j + 1) * COLS, :] * signs[m * 32 + j : m * 32 + j + 1, cut]
+            answers += [total[:, :LANES], total[:, LANES:]]
+    answers = jnp.concatenate([answer * factor for answer, factor in zip(answers, factors)], axis=0)
+    reply[...] = jnp.concatenate([answers, pltpu.roll(answers, CHIPS, 1)], axis=0).T[:CHIPS]
+
+
+def answer_other_kernel(message, reply, left, right, signs):
     for half in range(HALVES):
         for pair in range(CHIPS // 2):
             tile = jnp.concatenate(
@@ -187,23 +206,11 @@
             high, low = split(tile)
             left[half, pl.ds(pair * 16, 16), :LANES] = high
             left[half, pl.ds(pair * 16, 16), LANES:] = low
-    answers = []
-    width = 256
-    for half in range(HALVES):
-        for n in range(PICKS // width):
-            cut = slice(half * PICKS + n * width, half * PICKS + (n + 1) * width)
-            total = jnp.zeros((COLS, width), jnp.float32)
-            for m in range(2):
-                part = jnp.dot(
-                    left[half, m * 256 : (m + 1) * 256, :], right[:, cut], preferred_element_type=jnp.float32
-                )
-                for j in range(32):
-                    total = total + part[j * COLS : (j + 1) * COLS, :] * signs[m * 32 + j : m * 32 + j + 1, cut]
-            answers += [total[:, :LANES], total[:, LANES:]]
-    answers = [answer * factor for answer, factor in zip(answers, factors)]
-    answers = jnp.concatenate(answers, axis=0).T
-    mine[...] = answers[:CHIPS, :]
-    theirs[...] = answers[CHIPS:, :]
+    answer(message, 1, left, reply, right, signs)
+
+
+def answer_own_kernel(message, left, reply, right, signs):
+    answer(message, 0, left, reply, right, signs)
 
 
 def finish_kernel(reply, slots, sketch_hbm, gram_hbm, sketch, gram, sent):
@@ -242,21 +249,16 @@
     owners_other = other_core(owners)
     offsets_other = other_core(offsets)
     message_shape = jax.ShapeDtypeStruct((CHIPS * CHUNK, LANES), f32)
-    message, own, slots = pl.pallas_call(
+    picks_shape = jax.ShapeDtypeStruct((1, PICKS), i32)
+    message, owners, offsets = pl.pallas_call(
         send_kernel,
         name="transform_sections",
-        out_shape=(
-            message_shape,
-            jax.ShapeDtypeStruct((CHIPS, LANES), f32),
-            jax.ShapeDtypeStruct((1, PICKS), i32),
-        ),
+        out_shape=(message_shape, picks_shape, picks_shape),
         in_specs=[HBM] * 4,
         out_specs=(VMEM, VMEM, VMEM),
         scratch_shapes=[
             pltpu.VMEM((COLS, LANES * LANES), f32),
             pltpu.VMEM((LANES, LANES), i32),
-            pltpu.VMEM((1, PICKS), i32),
-            pltpu.VMEM((1, PICKS), i32),
             pltpu.VMEM((LANES, COLS, LANES), f32),
             pltpu.SemaphoreType.DMA((3 + PIECES,)),
         ],
@@ -268,31 +270,39 @@
             for operand in (matrix, flips.reshape(LANES, LANES), owners, offsets)
         )
     )
-    message = pl.pallas_call(
+    message, slots = pl.pallas_call(
         ask_kernel,
-        name="other_requests",
-        out_shape=message_shape,
-        in_specs=[VMEM] * 4,
-        out_specs=VMEM,
+        name="requests",
+        out_shape=(message_shape, picks_shape),
+        in_specs=[VMEM] * 5,
+        out_specs=(VMEM, VMEM),
         input_output_aliases={0: 0},
         compiler_params=params,
-    )(message, own, owners_other, offsets_other)
+    )(message, owners, offsets, owners_other, offsets_other)
     message = exchange(message)
-    half_shape = jax.ShapeDtypeStruct((CHIPS, LANES), f32)
-    mine, theirs = pl.pallas_call(
-        answer_kernel,
-        name="answer",
-        out_shape=(half_shape, half_shape),
+    reply_shape = jax.ShapeDtypeStruct((CHIPS, LANES), f32)
+    tables = [pltpu.VMEM((2 * LANES, PICKS), jnp.bfloat16), pltpu.VMEM((CHIPS, PICKS), f32)]
+    theirs, left = pl.pallas_call(
+        answer_other_kernel,
+        name="answer_other",
+        out_shape=(reply_shape, jax.ShapeDtypeStruct((HALVES, CHIPS * COLS, 2 * LANES), jnp.bfloat16)),
         in_specs=[VMEM],
         out_specs=(VMEM, VMEM),
-        scratch_shapes=[
-            pltpu.VMEM((HALVES, CHIPS * COLS, 2 * LANES), jnp.bfloat16),
-            pltpu.VMEM((2 * LANES, HALVES * PICKS), jnp.bfloat16),
-            pltpu.VMEM((CHIPS, HALVES * PICKS), f32),
-        ],
+        scratch_shapes=tables,
         compiler_params=params,
     )(message)
-    reply = exchange(mine + other_core(theirs))
+    theirs = other_core(theirs)
+    mine = pl.pallas_call(
+        answer_own_kernel,
+        name="answer_own",
+        out_shape=reply_shape,
+        in_specs=[VMEM, VMEM],
+        out_specs=VMEM,
+        scratch_shapes=tables,
+        compiler_params=params,
+        cost_estimate=pl.CostEstimate(flops=2**28, bytes_accessed=2**21, transcendentals=0),
+    )(message, left)
+    reply = exchange(mine + theirs)
     sketch, gram = pl.pallas_call(
         finish_kernel,
         name="finish",

time: 41.2 us -> 40.8 us (level)
  waiting for transfers between devices: 0.87 us -> 0.14 us
    ppermute x3, waiting for transfers between devices: 0.87 us -> 0.14 us  [other_core(): return lax.ppermute(value, 'all', [(i, i ^ 4) for i in range(2 * CHIPS)])]
    pallas_call x2 -> x3, Pallas kernels: 1.75 us -> 2.31 us  [the longest x1 0.85 us: on_device(): pl.pallas_call(ask_kernel, name='requests', out_shape=(message_shape, pic...]
    all_to_all x2, blocking collectives: 32 us -> 31.6 us  [exchange(): lax.all_to_all(parts, 'all', split_axis=0, concat_axis=0, tiled=True, axi...]
  transfers between devices with their start and end apart: 3 -> 3, of which waited for: 1 -> 1; matrix products, arithmetic and copies ran while one was open for 0% -> 0% of each run, Pallas kernels for 4% -> 5%
where the time goes in v5:
time: 40.8 us; the launch traced here: 40.2 us
  blocking collectives  31.6 us (77%)
  Pallas kernels  4.56 us (11%)
  starting transfers between devices  3.21 us (8%)
  between operations  0.67 us (2%)
    all_to_all x2, blocking collectives, exchange(): lax.all_to_all(parts, 'all', split_axis=0, concat_axis=0, tiled=True, axi...  31.6 us
    ppermute x3, starting transfers between devices, other_core(): return lax.ppermute(value, 'all', [(i, i ^ 4) for i in range(2 * CHIPS)])  3.21 us
    pallas_call x1, Pallas kernels, on_device(): pl.pallas_call(send_kernel, name='transform_sections', out_shape=(message...  1.32 us
    pallas_call x1, Pallas kernels, on_device(): pl.pallas_call(finish_kernel, name='finish', out_shape=(jax.ShapeDtypeStr...  0.93 us
    pallas_call x1, Pallas kernels, on_device(): pl.pallas_call(ask_kernel, name='requests', out_shape=(message_shape, pic...  0.85 us
  transfers between devices with their start and end apart: 3, of which 1 were waited for; matrix products, arithmetic and copies ran while one was open for 0% of the time, Pallas kernels for 5%

profile of v5, /device:TPU:1, one launch (start us, length us, event | category | flops | bytes accessed | tf_op | source)
XLA Modules:
  0.0 40.2 jit_solution(1298730275231414828)
XLA Ops:
  0.6 1.5 %collective-permute-start = (s32[1,1024]{1,0:T(1,128)}, s32[1,1024]{1,0:T(1,128)S(1)}, u32[]{:S(2)}, u32[]{:S(2)}) collective-permute-start(s32[1,1024]{1,0:T(1,128)} %bitcast.16), channel_id=1, source_target_pairs={{0,4},{1,5},{2,6},{3,7},{4,0},{5,1},{6,2},{7,3},{8,12},{9,13},{10,... | collective-permute-start | bytes 12296 | tf_op jit(solution)/shard_map/ppermute | solution.py:36
  2.1 0.1 collective-permute-start.1
  2.2 1.3 %transform_sections.1 = (f32[1088,128]{1,0:T(8,128)S(1)}, s32[1,1024]{1,0:T(1,128)S(1)}, s32[1,1024]{1,0:T(1,128)S(1)}) custom-call(f32[8,16384]{1,0:T(8,128)} %matrix_hbm.1, s32[128,128]{1,0:T(8,128)} %bitcast.15, s32[1,1024]{1,0:T(1,128)} %bitcast.17, s32[1,1024]{1,0:T(1,128)} %bitcast.19), custom_call_target="tpu_custom_call" | custom-call | flops 4194304 | bytes 4194304 | tf_op jit(solution)/shard_map/transform_sections/pallas_call | solution.py:253
  3.6 0.0 collective-permute-done.owners_other
  3.6 0.0 collective-permute-done.1.offsets_other
  3.6 0.8 %requests.1 = (f32[1088,128]{1,0:T(8,128)S(1)}, s32[1,1024]{1,0:T(1,128)S(1)}) custom-call(f32[1088,128]{1,0:T(8,128)S(1)} %get-tuple-element.11._, s32[1,1024]{1,0:T(1,128)S(1)} %get-tuple-element.12.owners, s32[1,1024]{1,0:T(1,128)S(1)} %get-tuple-element.13.offsets, ...), custom_call_target="tpu_custom_call", output_to_operand_aliasing={{0}: (0, {})} | custom-call | tf_op jit(solution)/shard_map/requests/pallas_call | solution.py:273
  4.4 19.2 %all_to_all.10 = f32[64,1,2176]{2,1,0:T(1,128)S(1)} all-to-all(f32[64,1,2176]{2,1,0:T(1,128)S(1)} %bitcast.12), channel_id=1, replica_groups={{90,91,88,89,82,83,80,81,74,75,72,73,66,67,64,65,122,123,120,121,114,11..., dimensions={0} | all-to-all | bytes 1114112 | tf_op jit(solution)/shard_map/all_to_all | solution.py:31
  23.6 0.7 %answer_other.1 = (f32[64,128]{1,0:T(8,128)S(1)}, bf16[2,512,256]{2,1,0:T(8,128)(2,1)S(1)}) custom-call(f32[1088,128]{1,0:T(8,128)S(1)} %bitcast.10), custom_call_target="tpu_custom_call" | custom-call | tf_op jit(solution)/shard_map/answer_other/pallas_call | solution.py:285
  24.3 1.6 %collective-permute-start.2 = (f32[64,128]{1,0:T(8,128)S(1)}, f32[64,128]{1,0:T(8,128)S(1)}, u32[]{:S(2)}, u32[]{:S(2)}) collective-permute-start(f32[64,128]{1,0:T(8,128)S(1)} %get-tuple-element.16), channel_id=1, source_target_pairs={{0,4},{1,5},{2,6},{3,7},{4,0},{5,1},{6,2},{7,3},{8,12},{9,13},{10,... | collective-permute-start | bytes 98312 | tf_op jit(solution)/shard_map/ppermute | solution.py:36
  25.9 0.7 %answer_own.1 = f32[64,128]{1,0:T(8,128)S(1)} custom-call(f32[1088,128]{1,0:T(8,128)S(1)} %bitcast.11, bf16[2,512,256]{2,1,0:T(8,128)(2,1)S(1)} %get-tuple-element.15.left), custom_call_target="tpu_custom_call" | custom-call | flops 268435456 | bytes 2097152 | tf_op jit(solution)/shard_map/answer_own/pallas_call | solution.py:295
  26.7 0.1 collective-permute-done.2
  26.8 12.5 %all_to_all.11 = f32[64,1,128]{2,1,0:T(1,128)S(1)} all-to-all(f32[64,1,128]{2,1,0:T(1,128)S(1)} %bitcast.14), channel_id=1, replica_groups={{90,91,88,89,82,83,80,81,74,75,72,73,66,67,64,65,122,123,120,121,114,11..., dimensions={0} | all-to-all | bytes 65536 | tf_op jit(solution)/shard_map/all_to_all | solution.py:31
  39.3 0.9 %finish.1 = (f32[8,1024]{1,0:T(8,128)}, f32[1,64]{1,0:T(1,128)}) custom-call(f32[64,128]{1,0:T(8,128)S(1)} %bitcast.13, s32[1,1024]{1,0:T(1,128)S(1)} %get-tuple-element.17.slots), custom_call_target="tpu_custom_call" | custom-call | tf_op jit(solution)/shard_map/finish/pallas_call | solution.py:306
  (1 shorter events, 0.0 us)
Async XLA Ops:
  0.6 2.9 %collective-permute-start = (s32[1,1024]{1,0:T(1,128)}, s32[1,1024]{1,0:T(1,128)S(1)}, u32[]{:S(2)}, u32[]{:S(2)}) collective-permute-start(s32[1,1024]{1,0:T(1,128)} %bitcast.16), channel_id=1, source_target_pairs={{0,4},{1,5},{2,6},{3,7},{4,0},{5,1},{6,2},{7,3},{8,12},{9,13},{10,... | collective-permute-start | bytes 12296 | tf_op jit(solution)/shard_map/ppermute | solution.py:36
  2.1 1.4 %collective-permute-start.1 = (s32[1,1024]{1,0:T(1,128)}, s32[1,1024]{1,0:T(1,128)S(1)}, u32[]{:S(2)}, u32[]{:S(2)}) collective-permute-start(s32[1,1024]{1,0:T(1,128)} %bitcast.18), channel_id=1, source_target_pairs={{0,4},{1,5},{2,6},{3,7},{4,0},{5,1},{6,2},{7,3},{8,12},{9,13},{10,... | collective-permute-start | bytes 12296 | tf_op jit(solution)/shard_map/ppermute | solution.py:36
  24.3 2.5 %collective-permute-start.2 = (f32[64,128]{1,0:T(8,128)S(1)}, f32[64,128]{1,0:T(8,128)S(1)}, u32[]{:S(2)}, u32[]{:S(2)}) collective-permute-start(f32[64,128]{1,0:T(8,128)S(1)} %get-tuple-element.16), channel_id=1, source_target_pairs={{0,4},{1,5},{2,6},{3,7},{4,0},{5,1},{6,2},{7,3},{8,12},{9,13},{10,... | collective-permute-start | bytes 98312 | tf_op jit(solution)/shard_map/ppermute | solution.py:36

commit v6 on v5

--- a/solution.py
+++ b/solution.py
@@ -17,6 +17,7 @@
 PICKS = LANES * SLOTS
 PIECES = 4
 FIRST = 46
+FIRST_BACK = 42
 VMEM = pl.BlockSpec(memory_space=pltpu.VMEM)
 HBM = pl.BlockSpec(memory_space=pltpu.HBM)
 
@@ -25,8 +26,8 @@
     return (chip >> 2) * 8 + core * 4 + (chip & 3)
 
 
-def exchange(rows):
-    groups = [[device(j ^ FIRST, core) for j in range(CHIPS)] for core in range(2)]
+def exchange(rows, first):
+    groups = [[device(j ^ first, core) for j in range(CHIPS)] for core in range(2)]
     parts = rows.reshape(CHIPS, 1, -1)
     parts = lax.all_to_all(parts, "all", split_axis=0, concat_axis=0, tiled=True, axis_index_groups=groups)
     return parts.reshape(rows.shape)
@@ -137,7 +138,7 @@
     rows = jnp.concatenate([rows, rows_other, rest], axis=0).T
     message[pl.ds(CHUNK - 1, CHIPS, stride=CHUNK), :] = rows[:CHIPS]
     section = lax.shift_right_logical(place, 7)
-    part = lax.shift_right_logical(section, 1) ^ FIRST
+    part = lax.shift_right_logical(section, 1) ^ FIRST_BACK
     slot = (section & 1) * SLOTS + rank
     slots[...] = part * (HALVES * SLOTS) + (slot & 1) * SLOTS + lax.shift_right_logical(slot, 1)
 
@@ -158,10 +159,16 @@
     return jnp.concatenate(blocks, axis=0)
 
 
+def reorder(rows, flip):
+    tiles = [rows[8 * i : 8 * i + 8] for i in range(rows.shape[0] // 8)]
+    tiles = [tiles[i ^ (flip >> 3)] for i in range(len(tiles))]
+    return jnp.concatenate([pltpu.roll(tile, 4, 0) if flip & 4 else tile for tile in tiles], axis=0)
+
+
 def answer(message, kind, left, reply, right, signs):
     core = lax.shift_right_logical(lax.axis_index("all"), 2) & 1
     count = HALVES * SLOTS
-    wanted = message[pl.ds(CHUNK - 1, CHIPS, stride=CHUNK), :]
+    wanted = reorder(message[pl.ds(CHUNK - 1, CHIPS, stride=CHUNK), :], FIRST ^ FIRST_BACK)
     even, odd = [(LANES - kind * count - n) % LANES for n in range(2)]
     wanted = jnp.concatenate([pltpu.roll(wanted, even, 1) if even else wanted, pltpu.roll(wanted, odd, 1)], axis=0)
     wanted = wanted.T[:count, :].astype(jnp.int32)
@@ -279,7 +286,7 @@
         input_output_aliases={0: 0},
         compiler_params=params,
     )(message, owners, offsets, owners_other, offsets_other)
-    message = exchange(message)
+    message = exchange(message, FIRST)
     reply_shape = jax.ShapeDtypeStruct((CHIPS, LANES), f32)
     tables = [pltpu.VMEM((2 * LANES, PICKS), jnp.bfloat16), pltpu.VMEM((CHIPS, PICKS), f32)]
     theirs, left = pl.pallas_call(
@@ -302,7 +309,7 @@
         compiler_params=params,
         cost_estimate=pl.CostEstimate(flops=2**28, bytes_accessed=2**21, transcendentals=0),
     )(message, left)
-    reply = exchange(mine + theirs)
+    reply = exchange(mine + theirs, FIRST_BACK)
     sketch, gram = pl.pallas_call(
         finish_kernel,
         name="finish",

time: 40.8 us -> 40.2 us (0.985)
  blocking collectives: 31.6 us -> 31.1 us
    all_to_all x2, blocking collectives: 31.6 us -> 31.1 us  [exchange(): lax.all_to_all(parts, 'all', split_axis=0, concat_axis=0, tiled=True, axi...]
where the time goes in v6:
time: 40.2 us; the launch traced here: 39.7 us
  blocking collectives  31.1 us (77%)
  Pallas kernels  4.56 us (11%)
  starting transfers between devices  3.21 us (8%)
  between operations  0.67 us (2%)
    all_to_all x2, blocking collectives, exchange(): lax.all_to_all(parts, 'all', split_axis=0, concat_axis=0, tiled=True, axi...  31.1 us
    ppermute x3, starting transfers between devices, other_core(): return lax.ppermute(value, 'all', [(i, i ^ 4) for i in range(2 * CHIPS)])  3.21 us
    pallas_call x1, Pallas kernels, on_device(): pl.pallas_call(send_kernel, name='transform_sections', out_shape=(message...  1.32 us
    pallas_call x1, Pallas kernels, on_device(): pl.pallas_call(finish_kernel, name='finish', out_shape=(jax.ShapeDtypeStr...  0.93 us
    pallas_call x1, Pallas kernels, on_device(): pl.pallas_call(ask_kernel, name='requests', out_shape=(message_shape, pic...  0.85 us
  transfers between devices with their start and end apart: 3, of which 1 were waited for; matrix products, arithmetic and copies ran while one was open for 0% of the time, Pallas kernels for 5%

profile of v6, /device:TPU:1, one launch (start us, length us, event | category | flops | bytes accessed | tf_op | source)
XLA Modules:
  0.0 39.7 jit_solution(5617012145597594683)
XLA Ops:
  0.6 1.5 %collective-permute-start = (s32[1,1024]{1,0:T(1,128)}, s32[1,1024]{1,0:T(1,128)S(1)}, u32[]{:S(2)}, u32[]{:S(2)}) collective-permute-start(s32[1,1024]{1,0:T(1,128)} %bitcast.16), channel_id=1, source_target_pairs={{0,4},{1,5},{2,6},{3,7},{4,0},{5,1},{6,2},{7,3},{8,12},{9,13},{10,... | collective-permute-start | bytes 12296 | tf_op jit(solution)/shard_map/ppermute | solution.py:37
  2.1 0.1 collective-permute-start.1
  2.2 1.3 %transform_sections.1 = (f32[1088,128]{1,0:T(8,128)S(1)}, s32[1,1024]{1,0:T(1,128)S(1)}, s32[1,1024]{1,0:T(1,128)S(1)}) custom-call(f32[8,16384]{1,0:T(8,128)} %matrix_hbm.1, s32[128,128]{1,0:T(8,128)} %bitcast.15, s32[1,1024]{1,0:T(1,128)} %bitcast.17, s32[1,1024]{1,0:T(1,128)} %bitcast.19), custom_call_target="tpu_custom_call" | custom-call | flops 4194304 | bytes 4194304 | tf_op jit(solution)/shard_map/transform_sections/pallas_call | solution.py:260
  3.6 0.0 collective-permute-done.owners_other
  3.6 0.0 collective-permute-done.1.offsets_other
  3.6 0.8 %requests.1 = (f32[1088,128]{1,0:T(8,128)S(1)}, s32[1,1024]{1,0:T(1,128)S(1)}) custom-call(f32[1088,128]{1,0:T(8,128)S(1)} %get-tuple-element.11._, s32[1,1024]{1,0:T(1,128)S(1)} %get-tuple-element.12.owners, s32[1,1024]{1,0:T(1,128)S(1)} %get-tuple-element.13.offsets, ...), custom_call_target="tpu_custom_call", output_to_operand_aliasing={{0}: (0, {})} | custom-call | tf_op jit(solution)/shard_map/requests/pallas_call | solution.py:280
  4.4 19.2 %all_to_all.10 = f32[64,1,2176]{2,1,0:T(1,128)S(1)} all-to-all(f32[64,1,2176]{2,1,0:T(1,128)S(1)} %bitcast.12), channel_id=1, replica_groups={{90,91,88,89,82,83,80,81,74,75,72,73,66,67,64,65,122,123,120,121,114,11..., dimensions={0} | all-to-all | bytes 1114112 | tf_op jit(solution)/shard_map/all_to_all | solution.py:32
  23.6 0.7 %answer_other.1 = (f32[64,128]{1,0:T(8,128)S(1)}, bf16[2,512,256]{2,1,0:T(8,128)(2,1)S(1)}) custom-call(f32[1088,128]{1,0:T(8,128)S(1)} %bitcast.10), custom_call_target="tpu_custom_call" | custom-call | tf_op jit(solution)/shard_map/answer_other/pallas_call | solution.py:292
  24.3 1.6 %collective-permute-start.2 = (f32[64,128]{1,0:T(8,128)S(1)}, f32[64,128]{1,0:T(8,128)S(1)}, u32[]{:S(2)}, u32[]{:S(2)}) collective-permute-start(f32[64,128]{1,0:T(8,128)S(1)} %get-tuple-element.16), channel_id=1, source_target_pairs={{0,4},{1,5},{2,6},{3,7},{4,0},{5,1},{6,2},{7,3},{8,12},{9,13},{10,... | collective-permute-start | bytes 98312 | tf_op jit(solution)/shard_map/ppermute | solution.py:37
  25.9 0.7 %answer_own.1 = f32[64,128]{1,0:T(8,128)S(1)} custom-call(f32[1088,128]{1,0:T(8,128)S(1)} %bitcast.11, bf16[2,512,256]{2,1,0:T(8,128)(2,1)S(1)} %get-tuple-element.15.left), custom_call_target="tpu_custom_call" | custom-call | flops 268435456 | bytes 2097152 | tf_op jit(solution)/shard_map/answer_own/pallas_call | solution.py:302
  26.7 0.1 collective-permute-done.2
  26.8 11.9 %all_to_all.11 = f32[64,1,128]{2,1,0:T(1,128)S(1)} all-to-all(f32[64,1,128]{2,1,0:T(1,128)S(1)} %bitcast.14), channel_id=1, replica_groups={{82,83,80,81,90,91,88,89,66,67,64,65,74,75,72,73,114,115,112,113,122,12..., dimensions={0} | all-to-all | bytes 65536 | tf_op jit(solution)/shard_map/all_to_all | solution.py:32
  38.7 0.9 %finish.1 = (f32[8,1024]{1,0:T(8,128)}, f32[1,64]{1,0:T(1,128)}) custom-call(f32[64,128]{1,0:T(8,128)S(1)} %bitcast.13, s32[1,1024]{1,0:T(1,128)S(1)} %get-tuple-element.17.slots), custom_call_target="tpu_custom_call" | custom-call | tf_op jit(solution)/shard_map/finish/pallas_call | solution.py:313
  (1 shorter events, 0.0 us)
Async XLA Ops:
  0.6 2.9 %collective-permute-start = (s32[1,1024]{1,0:T(1,128)}, s32[1,1024]{1,0:T(1,128)S(1)}, u32[]{:S(2)}, u32[]{:S(2)}) collective-permute-start(s32[1,1024]{1,0:T(1,128)} %bitcast.16), channel_id=1, source_target_pairs={{0,4},{1,5},{2,6},{3,7},{4,0},{5,1},{6,2},{7,3},{8,12},{9,13},{10,... | collective-permute-start | bytes 12296 | tf_op jit(solution)/shard_map/ppermute | solution.py:37
  2.1 1.4 %collective-permute-start.1 = (s32[1,1024]{1,0:T(1,128)}, s32[1,1024]{1,0:T(1,128)S(1)}, u32[]{:S(2)}, u32[]{:S(2)}) collective-permute-start(s32[1,1024]{1,0:T(1,128)} %bitcast.18), channel_id=1, source_target_pairs={{0,4},{1,5},{2,6},{3,7},{4,0},{5,1},{6,2},{7,3},{8,12},{9,13},{10,... | collective-permute-start | bytes 12296 | tf_op jit(solution)/shard_map/ppermute | solution.py:37
  24.3 2.5 %collective-permute-start.2 = (f32[64,128]{1,0:T(8,128)S(1)}, f32[64,128]{1,0:T(8,128)S(1)}, u32[]{:S(2)}, u32[]{:S(2)}) collective-permute-start(f32[64,128]{1,0:T(8,128)S(1)} %get-tuple-element.16), channel_id=1, source_target_pairs={{0,4},{1,5},{2,6},{3,7},{4,0},{5,1},{6,2},{7,3},{8,12},{9,13},{10,... | collective-permute-start | bytes 98312 | tf_op jit(solution)/shard_map/ppermute | solution.py:37

commit v7 on v6

--- a/solution.py
+++ b/solution.py
@@ -95,8 +95,8 @@
     return rank, jnp.concatenate([rows, pltpu.roll(rows, CHIPS, 1)], axis=0)
 
 
-def send_kernel(
-    matrix_hbm, flips_hbm, owners_hbm, offsets_hbm, message, owners, offsets, matrix, flips, mid, arrived
+def load_kernel(
+    matrix_hbm, flips_hbm, owners_hbm, offsets_hbm, matrix, flips, own, slots, owners, offsets, arrived
 ):
     copies = [
         pltpu.make_async_copy(source, target, arrived.at[i])
@@ -110,12 +110,27 @@
         copies.append(pltpu.make_async_copy(matrix_hbm.at[:, cut], matrix.at[:, cut], arrived.at[3 + p]))
     for copy in copies:
         copy.start()
+    copies[1].wait()
+    copies[2].wait()
+    place = offsets[...]
+    rank, rows = requests(place, owners[...])
+    own[...] = rows
+    section = lax.shift_right_logical(place, 7)
+    part = lax.shift_right_logical(section, 1) ^ FIRST_BACK
+    slot = (section & 1) * SLOTS + rank
+    slots[...] = part * (HALVES * SLOTS) + (slot & 1) * SLOTS + lax.shift_right_logical(slot, 1)
+    for copy in [copies[0]] + copies[3:]:
+        copy.wait()
+
+
+def send_kernel(matrix, flips, own, owners, offsets, message, mid):
+    _, rows = requests(offsets[...], owners[...])
+    rest = jnp.zeros((LANES - 2 * HALVES * SLOTS, LANES), jnp.float32)
+    rows = jnp.concatenate([own[...], rows, rest], axis=0).T
+    message[pl.ds(CHUNK - 1, CHIPS, stride=CHUNK), :] = rows[:CHIPS]
     scale = 1.0 / math.sqrt(float(LANES) ** 3)
-    copies[0].wait()
     signs = jnp.where(flips[...] == 1, scale, -scale)
     for i in range(16):
-        if i * PIECES % 16 == 0:
-            copies[3 + i * PIECES // 16].wait()
         tiles = []
         for f in range(i * 8, i * 8 + 8):
             tiles.append(matrix[:, f * LANES : (f + 1) * LANES] * signs[f : f + 1, :])
@@ -126,21 +141,6 @@
             section = i * 8 + j
             row = ((section >> 1) ^ FIRST) * CHUNK + (section & 1) * COLS
             message[pl.ds(row, COLS), :] = tile
-    copies[1].wait()
-    copies[2].wait()
-
-
-def ask_kernel(_, owners, offsets, owners_other, offsets_other, message, slots):
-    place = offsets[...]
-    rank, rows = requests(place, owners[...])
-    _, rows_other = requests(offsets_other[...], owners_other[...])
-    rest = jnp.zeros((LANES - 2 * HALVES * SLOTS, LANES), jnp.float32)
-    rows = jnp.concatenate([rows, rows_other, rest], axis=0).T
-    message[pl.ds(CHUNK - 1, CHIPS, stride=CHUNK), :] = rows[:CHIPS]
-    section = lax.shift_right_logical(place, 7)
-    part = lax.shift_right_logical(section, 1) ^ FIRST_BACK
-    slot = (section & 1) * SLOTS + rank
-    slots[...] = part * (HALVES * SLOTS) + (slot & 1) * SLOTS + lax.shift_right_logical(slot, 1)
 
 
 def bit_sign(index, bit):
@@ -257,16 +257,20 @@
     offsets_other = other_core(offsets)
     message_shape = jax.ShapeDtypeStruct((CHIPS * CHUNK, LANES), f32)
     picks_shape = jax.ShapeDtypeStruct((1, PICKS), i32)
-    message, owners, offsets = pl.pallas_call(
-        send_kernel,
-        name="transform_sections",
-        out_shape=(message_shape, picks_shape, picks_shape),
+    matrix, flips, own, slots = pl.pallas_call(
+        load_kernel,
+        name="load_and_requests",
+        out_shape=(
+            jax.ShapeDtypeStruct((COLS, LANES * LANES), f32),
+            jax.ShapeDtypeStruct((LANES, LANES), i32),
+            jax.ShapeDtypeStruct((HALVES * SLOTS, LANES), f32),
+            picks_shape,
+        ),
         in_specs=[HBM] * 4,
-        out_specs=(VMEM, VMEM, VMEM),
+        out_specs=(VMEM, VMEM, VMEM, VMEM),
         scratch_shapes=[
-            pltpu.VMEM((COLS, LANES * LANES), f32),
-            pltpu.VMEM((LANES, LANES), i32),
-            pltpu.VMEM((LANES, COLS, LANES), f32),
+            pltpu.VMEM((1, PICKS), i32),
+            pltpu.VMEM((1, PICKS), i32),
             pltpu.SemaphoreType.DMA((3 + PIECES,)),
         ],
         compiler_params=params,
@@ -277,15 +281,15 @@
             for operand in (matrix, flips.reshape(LANES, LANES), owners, offsets)
         )
     )
-    message, slots = pl.pallas_call(
-        ask_kernel,
-        name="requests",
-        out_shape=(message_shape, picks_shape),
+    message = pl.pallas_call(
+        send_kernel,
+        name="transform_and_requests",
+        out_shape=message_shape,
         in_specs=[VMEM] * 5,
-        out_specs=(VMEM, VMEM),
-        input_output_aliases={0: 0},
-        compiler_params=params,
-    )(message, owners, offsets, owners_other, offsets_other)
+        out_specs=VMEM,
+        scratch_shapes=[pltpu.VMEM((LANES, COLS, LANES), f32)],
+        compiler_params=params,
+    )(matrix, flips, own, owners_other, offsets_other)
     message = exchange(message, FIRST)
     reply_shape = jax.ShapeDtypeStruct((CHIPS, LANES), f32)
     tables = [pltpu.VMEM((2 * LANES, PICKS), jnp.bfloat16), pltpu.VMEM((CHIPS, PICKS), f32)]

time: 40.2 us -> 40 us (level)
  no operation moved by 1% of the time
where the time goes in v7:
time: 40 us; the launch traced here: 39.5 us
  blocking collectives  31.1 us (78%)
  Pallas kernels  4.36 us (11%)
  starting transfers between devices  3.21 us (8%)
  between operations  0.68 us (2%)
    all_to_all x2, blocking collectives, exchange(): lax.all_to_all(parts, 'all', split_axis=0, concat_axis=0, tiled=True, axi...  31.1 us
    ppermute x3, starting transfers between devices, other_core(): return lax.ppermute(value, 'all', [(i, i ^ 4) for i in range(2 * CHIPS)])  3.21 us
    pallas_call x1, Pallas kernels, on_device(): pl.pallas_call(load_kernel, name='load_and_requests', out_shape=(jax.Shap...  1.31 us
    pallas_call x1, Pallas kernels, on_device(): pl.pallas_call(finish_kernel, name='finish', out_shape=(jax.ShapeDtypeStr...  0.93 us
  transfers between devices with their start and end apart: 3, of which 1 were waited for; matrix products, arithmetic and copies ran while one was open for 0% of the time, Pallas kernels for 5%

profile of v7, /device:TPU:1, one launch (start us, length us, event | category | flops | bytes accessed | tf_op | source)
XLA Modules:
  0.0 39.5 jit_solution(12390573417114220188)
XLA Ops:
  0.6 1.5 %collective-permute-start = (s32[1,1024]{1,0:T(1,128)}, s32[1,1024]{1,0:T(1,128)S(1)}, u32[]{:S(2)}, u32[]{:S(2)}) collective-permute-start(s32[1,1024]{1,0:T(1,128)} %bitcast.16), channel_id=1, source_target_pairs={{0,4},{1,5},{2,6},{3,7},{4,0},{5,1},{6,2},{7,3},{8,12},{9,13},{10,... | collective-permute-start | bytes 12296 | tf_op jit(solution)/shard_map/ppermute | solution.py:37
  2.1 0.1 collective-permute-start.1
  2.2 1.3 %load_and_requests.1 = (f32[8,16384]{1,0:T(8,128)S(1)}, s32[128,128]{1,0:T(8,128)S(1)}, f32[16,128]{1,0:T(8,128)S(1)}, s32[1,1024]{1,0:T(1,128)S(1)}) custom-call(f32[8,16384]{1,0:T(8,128)} %matrix_hbm.1, s32[128,128]{1,0:T(8,128)} %bitcast.15, s32[1,1024]{1,0:T(1,128)} %bitcast.17, s32[1,1024]{1,0:T(1,128)} %bitcast.19), custom_call_target="tpu_custom_call" | custom-call | flops 4194304 | bytes 4194304 | tf_op jit(solution)/shard_map/load_and_requests/pallas_call | solution.py:260
  3.5 0.0 collective-permute-done.owners
  3.6 0.0 collective-permute-done.1.offsets
  3.6 0.7 %transform_and_requests.1 = f32[1088,128]{1,0:T(8,128)S(1)} custom-call(f32[8,16384]{1,0:T(8,128)S(1)} %get-tuple-element.10.matrix, s32[128,128]{1,0:T(8,128)S(1)} %get-tuple-element.11.flips, f32[16,128]{1,0:T(8,128)S(1)} %get-tuple-element.12.own, s32[1,1024]{1,0:T(1,128)S(1)} %collective-permute-done.owners, s32[1,1024]{1,0:T(1,128)S(1)} %collective-permute-done.1.offsets), custom_call_target="tpu_custom_call" | custom-call | tf_op jit(solution)/shard_map/transform_and_requests/pallas_call | solution.py:284
  4.2 19.1 %all_to_all.10 = f32[64,1,2176]{2,1,0:T(1,128)S(1)} all-to-all(f32[64,1,2176]{2,1,0:T(1,128)S(1)} %bitcast.12), channel_id=1, replica_groups={{90,91,88,89,82,83,80,81,74,75,72,73,66,67,64,65,122,123,120,121,114,11..., dimensions={0} | all-to-all | bytes 1114112 | tf_op jit(solution)/shard_map/all_to_all | solution.py:32
  23.4 0.7 %answer_other.1 = (f32[64,128]{1,0:T(8,128)S(1)}, bf16[2,512,256]{2,1,0:T(8,128)(2,1)S(1)}) custom-call(f32[1088,128]{1,0:T(8,128)S(1)} %bitcast.10), custom_call_target="tpu_custom_call" | custom-call | tf_op jit(solution)/shard_map/answer_other/pallas_call | solution.py:296
  24.1 1.6 %collective-permute-start.2 = (f32[64,128]{1,0:T(8,128)S(1)}, f32[64,128]{1,0:T(8,128)S(1)}, u32[]{:S(2)}, u32[]{:S(2)}) collective-permute-start(f32[64,128]{1,0:T(8,128)S(1)} %get-tuple-element.14), channel_id=1, source_target_pairs={{0,4},{1,5},{2,6},{3,7},{4,0},{5,1},{6,2},{7,3},{8,12},{9,13},{10,... | collective-permute-start | bytes 98312 | tf_op jit(solution)/shard_map/ppermute | solution.py:37
  25.7 0.7 %answer_own.1 = f32[64,128]{1,0:T(8,128)S(1)} custom-call(f32[1088,128]{1,0:T(8,128)S(1)} %bitcast.11, bf16[2,512,256]{2,1,0:T(8,128)(2,1)S(1)} %get-tuple-element.13.left), custom_call_target="tpu_custom_call" | custom-call | flops 268435456 | bytes 2097152 | tf_op jit(solution)/shard_map/answer_own/pallas_call | solution.py:306
  26.5 0.1 collective-permute-done.2
  26.6 11.9 %all_to_all.11 = f32[64,1,128]{2,1,0:T(1,128)S(1)} all-to-all(f32[64,1,128]{2,1,0:T(1,128)S(1)} %bitcast.14), channel_id=1, replica_groups={{82,83,80,81,90,91,88,89,66,67,64,65,74,75,72,73,114,115,112,113,122,12..., dimensions={0} | all-to-all | bytes 65536 | tf_op jit(solution)/shard_map/all_to_all | solution.py:32
  38.5 0.9 %finish.1 = (f32[8,1024]{1,0:T(8,128)}, f32[1,64]{1,0:T(1,128)}) custom-call(f32[64,128]{1,0:T(8,128)S(1)} %bitcast.13, s32[1,1024]{1,0:T(1,128)S(1)} %get-tuple-element.15.slots), custom_call_target="tpu_custom_call" | custom-call | tf_op jit(solution)/shard_map/finish/pallas_call | solution.py:317
  (1 shorter events, 0.0 us)
Async XLA Ops:
  0.6 2.9 %collective-permute-start = (s32[1,1024]{1,0:T(1,128)}, s32[1,1024]{1,0:T(1,128)S(1)}, u32[]{:S(2)}, u32[]{:S(2)}) collective-permute-start(s32[1,1024]{1,0:T(1,128)} %bitcast.16), channel_id=1, source_target_pairs={{0,4},{1,5},{2,6},{3,7},{4,0},{5,1},{6,2},{7,3},{8,12},{9,13},{10,... | collective-permute-start | bytes 12296 | tf_op jit(solution)/shard_map/ppermute | solution.py:37
  2.1 1.4 %collective-permute-start.1 = (s32[1,1024]{1,0:T(1,128)}, s32[1,1024]{1,0:T(1,128)S(1)}, u32[]{:S(2)}, u32[]{:S(2)}) collective-permute-start(s32[1,1024]{1,0:T(1,128)} %bitcast.18), channel_id=1, source_target_pairs={{0,4},{1,5},{2,6},{3,7},{4,0},{5,1},{6,2},{7,3},{8,12},{9,13},{10,... | collective-permute-start | bytes 12296 | tf_op jit(solution)/shard_map/ppermute | solution.py:37
  24.1 2.5 %collective-permute-start.2 = (f32[64,128]{1,0:T(8,128)S(1)}, f32[64,128]{1,0:T(8,128)S(1)}, u32[]{:S(2)}, u32[]{:S(2)}) collective-permute-start(f32[64,128]{1,0:T(8,128)S(1)} %get-tuple-element.14), channel_id=1, source_target_pairs={{0,4},{1,5},{2,6},{3,7},{4,0},{5,1},{6,2},{7,3},{8,12},{9,13},{10,... | collective-permute-start | bytes 98312 | tf_op jit(solution)/shard_map/ppermute | solution.py:37

commit v8 on v7

--- a/solution.py
+++ b/solution.py
@@ -15,7 +15,7 @@
 COLS = 8
 CHUNK = HALVES * COLS + 1
 PICKS = LANES * SLOTS
-PIECES = 4
+PIECES = 1
 FIRST = 46
 FIRST_BACK = 42
 VMEM = pl.BlockSpec(memory_space=pltpu.VMEM)
@@ -108,7 +108,7 @@
     for p in range(PIECES):
         cut = pl.ds(p * width, width)
         copies.append(pltpu.make_async_copy(matrix_hbm.at[:, cut], matrix.at[:, cut], arrived.at[3 + p]))
-    for copy in copies:
+    for copy in copies[2:0:-1] + copies[3:] + copies[:1]:
         copy.start()
     copies[1].wait()
     copies[2].wait()
@@ -125,9 +125,9 @@
 
 def send_kernel(matrix, flips, own, owners, offsets, message, mid):
     _, rows = requests(offsets[...], owners[...])
-    rest = jnp.zeros((LANES - 2 * HALVES * SLOTS, LANES), jnp.float32)
-    rows = jnp.concatenate([own[...], rows, rest], axis=0).T
-    message[pl.ds(CHUNK - 1, CHIPS, stride=CHUNK), :] = rows[:CHIPS]
+    rest = jnp.zeros((CHIPS, LANES - 2 * HALVES * SLOTS), jnp.float32)
+    rows = jnp.concatenate([own[...], rows], axis=0).T[:CHIPS]
+    message[pl.ds(CHUNK - 1, CHIPS, stride=CHUNK), :] = jnp.concatenate([rows, rest], axis=1)
     scale = 1.0 / math.sqrt(float(LANES) ** 3)
     signs = jnp.where(flips[...] == 1, scale, -scale)
     for i in range(16):
@@ -171,7 +171,7 @@
     wanted = reorder(message[pl.ds(CHUNK - 1, CHIPS, stride=CHUNK), :], FIRST ^ FIRST_BACK)
     even, odd = [(LANES - kind * count - n) % LANES for n in range(2)]
     wanted = jnp.concatenate([pltpu.roll(wanted, even, 1) if even else wanted, pltpu.roll(wanted, odd, 1)], axis=0)
-    wanted = wanted.T[:count, :].astype(jnp.int32)
+    wanted = wanted[:, :count].T.astype(jnp.int32)
     factors = []
     for n in range(count // 2):
         index = wanted[2 * n : 2 * n + 1, :]

time: 40 us -> 39.9 us (level)
  no operation moved by 1% of the time
where the time goes in v8:
time: 39.9 us; the launch traced here: 39.4 us
  blocking collectives  31 us (78%)
  Pallas kernels  4.31 us (11%)
  starting transfers between devices  3.21 us (8%)
  between operations  0.67 us (2%)
    all_to_all x2, blocking collectives, exchange(): lax.all_to_all(parts, 'all', split_axis=0, concat_axis=0, tiled=True, axi...  31 us
    ppermute x3, starting transfers between devices, other_core(): return lax.ppermute(value, 'all', [(i, i ^ 4) for i in range(2 * CHIPS)])  3.21 us
    pallas_call x1, Pallas kernels, on_device(): pl.pallas_call(load_kernel, name='load_and_requests', out_shape=(jax.Shap...  1.25 us
    pallas_call x1, Pallas kernels, on_device(): pl.pallas_call(finish_kernel, name='finish', out_shape=(jax.ShapeDtypeStr...  0.93 us
  transfers between devices with their start and end apart: 3, of which 1 were waited for; matrix products, arithmetic and copies ran while one was open for 0% of the time, Pallas kernels for 5%

profile of v8, /device:TPU:1, one launch (start us, length us, event | category | flops | bytes accessed | tf_op | source)
XLA Modules:
  0.0 39.4 jit_solution(6726975575561217202)
XLA Ops:
  0.6 1.5 %collective-permute-start = (s32[1,1024]{1,0:T(1,128)}, s32[1,1024]{1,0:T(1,128)S(1)}, u32[]{:S(2)}, u32[]{:S(2)}) collective-permute-start(s32[1,1024]{1,0:T(1,128)} %bitcast.16), channel_id=1, source_target_pairs={{0,4},{1,5},{2,6},{3,7},{4,0},{5,1},{6,2},{7,3},{8,12},{9,13},{10,... | collective-permute-start | bytes 12296 | tf_op jit(solution)/shard_map/ppermute | solution.py:37
  2.1 0.1 collective-permute-start.1
  2.2 1.2 %load_and_requests.1 = (f32[8,16384]{1,0:T(8,128)S(1)}, s32[128,128]{1,0:T(8,128)S(1)}, f32[16,128]{1,0:T(8,128)S(1)}, s32[1,1024]{1,0:T(1,128)S(1)}) custom-call(f32[8,16384]{1,0:T(8,128)} %matrix_hbm.1, s32[128,128]{1,0:T(8,128)} %bitcast.15, s32[1,1024]{1,0:T(1,128)} %bitcast.17, s32[1,1024]{1,0:T(1,128)} %bitcast.19), custom_call_target="tpu_custom_call" | custom-call | flops 4194304 | bytes 4194304 | tf_op jit(solution)/shard_map/load_and_requests/pallas_call | solution.py:260
  3.5 0.0 collective-permute-done.owners
  3.5 0.0 collective-permute-done.1.offsets
  3.5 0.7 %transform_and_requests.1 = f32[1088,128]{1,0:T(8,128)S(1)} custom-call(f32[8,16384]{1,0:T(8,128)S(1)} %get-tuple-element.10.matrix, s32[128,128]{1,0:T(8,128)S(1)} %get-tuple-element.11.flips, f32[16,128]{1,0:T(8,128)S(1)} %get-tuple-element.12.own, s32[1,1024]{1,0:T(1,128)S(1)} %collective-permute-done.owners, s32[1,1024]{1,0:T(1,128)S(1)} %collective-permute-done.1.offsets), custom_call_target="tpu_custom_call" | custom-call | tf_op jit(solution)/shard_map/transform_and_requests/pallas_call | solution.py:284
  4.2 19.1 %all_to_all.10 = f32[64,1,2176]{2,1,0:T(1,128)S(1)} all-to-all(f32[64,1,2176]{2,1,0:T(1,128)S(1)} %bitcast.12), channel_id=1, replica_groups={{90,91,88,89,82,83,80,81,74,75,72,73,66,67,64,65,122,123,120,121,114,11..., dimensions={0} | all-to-all | bytes 1114112 | tf_op jit(solution)/shard_map/all_to_all | solution.py:32
  23.3 0.7 %answer_other.1 = (f32[64,128]{1,0:T(8,128)S(1)}, bf16[2,512,256]{2,1,0:T(8,128)(2,1)S(1)}) custom-call(f32[1088,128]{1,0:T(8,128)S(1)} %bitcast.10), custom_call_target="tpu_custom_call" | custom-call | tf_op jit(solution)/shard_map/answer_other/pallas_call | solution.py:296
  24.1 1.6 %collective-permute-start.2 = (f32[64,128]{1,0:T(8,128)S(1)}, f32[64,128]{1,0:T(8,128)S(1)}, u32[]{:S(2)}, u32[]{:S(2)}) collective-permute-start(f32[64,128]{1,0:T(8,128)S(1)} %get-tuple-element.14), channel_id=1, source_target_pairs={{0,4},{1,5},{2,6},{3,7},{4,0},{5,1},{6,2},{7,3},{8,12},{9,13},{10,... | collective-permute-start | bytes 98312 | tf_op jit(solution)/shard_map/ppermute | solution.py:37
  25.7 0.7 %answer_own.1 = f32[64,128]{1,0:T(8,128)S(1)} custom-call(f32[1088,128]{1,0:T(8,128)S(1)} %bitcast.11, bf16[2,512,256]{2,1,0:T(8,128)(2,1)S(1)} %get-tuple-element.13.left), custom_call_target="tpu_custom_call" | custom-call | flops 268435456 | bytes 2097152 | tf_op jit(solution)/shard_map/answer_own/pallas_call | solution.py:306
  26.4 0.1 collective-permute-done.2
  26.6 11.9 %all_to_all.11 = f32[64,1,128]{2,1,0:T(1,128)S(1)} all-to-all(f32[64,1,128]{2,1,0:T(1,128)S(1)} %bitcast.14), channel_id=1, replica_groups={{82,83,80,81,90,91,88,89,66,67,64,65,74,75,72,73,114,115,112,113,122,12..., dimensions={0} | all-to-all | bytes 65536 | tf_op jit(solution)/shard_map/all_to_all | solution.py:32
  38.5 0.9 %finish.1 = (f32[8,1024]{1,0:T(8,128)}, f32[1,64]{1,0:T(1,128)}) custom-call(f32[64,128]{1,0:T(8,128)S(1)} %bitcast.13, s32[1,1024]{1,0:T(1,128)S(1)} %get-tuple-element.15.slots), custom_call_target="tpu_custom_call" | custom-call | tf_op jit(solution)/shard_map/finish/pallas_call | solution.py:317
  (1 shorter events, 0.0 us)
Async XLA Ops:
  0.6 2.9 %collective-permute-start = (s32[1,1024]{1,0:T(1,128)}, s32[1,1024]{1,0:T(1,128)S(1)}, u32[]{:S(2)}, u32[]{:S(2)}) collective-permute-start(s32[1,1024]{1,0:T(1,128)} %bitcast.16), channel_id=1, source_target_pairs={{0,4},{1,5},{2,6},{3,7},{4,0},{5,1},{6,2},{7,3},{8,12},{9,13},{10,... | collective-permute-start | bytes 12296 | tf_op jit(solution)/shard_map/ppermute | solution.py:37
  2.1 1.4 %collective-permute-start.1 = (s32[1,1024]{1,0:T(1,128)}, s32[1,1024]{1,0:T(1,128)S(1)}, u32[]{:S(2)}, u32[]{:S(2)}) collective-permute-start(s32[1,1024]{1,0:T(1,128)} %bitcast.18), channel_id=1, source_target_pairs={{0,4},{1,5},{2,6},{3,7},{4,0},{5,1},{6,2},{7,3},{8,12},{9,13},{10,... | collective-permute-start | bytes 12296 | tf_op jit(solution)/shard_map/ppermute | solution.py:37
  24.1 2.5 %collective-permute-start.2 = (f32[64,128]{1,0:T(8,128)S(1)}, f32[64,128]{1,0:T(8,128)S(1)}, u32[]{:S(2)}, u32[]{:S(2)}) collective-permute-start(f32[64,128]{1,0:T(8,128)S(1)} %get-tuple-element.14), channel_id=1, source_target_pairs={{0,4},{1,5},{2,6},{3,7},{4,0},{5,1},{6,2},{7,3},{8,12},{9,13},{10,... | collective-permute-start | bytes 98312 | tf_op jit(solution)/shard_map/ppermute | solution.py:37

commit v9 on v8

--- a/solution.py
+++ b/solution.py
@@ -165,14 +165,14 @@
     return jnp.concatenate([pltpu.roll(tile, 4, 0) if flip & 4 else tile for tile in tiles], axis=0)
 
 
-def answer(message, kind, left, reply, right, signs):
+def answer(message, kind, left, reply, right):
     core = lax.shift_right_logical(lax.axis_index("all"), 2) & 1
     count = HALVES * SLOTS
     wanted = reorder(message[pl.ds(CHUNK - 1, CHIPS, stride=CHUNK), :], FIRST ^ FIRST_BACK)
     even, odd = [(LANES - kind * count - n) % LANES for n in range(2)]
     wanted = jnp.concatenate([pltpu.roll(wanted, even, 1) if even else wanted, pltpu.roll(wanted, odd, 1)], axis=0)
     wanted = wanted[:, :count].T.astype(jnp.int32)
-    factors = []
+    factors, spread = [], []
     for n in range(count // 2):
         index = wanted[2 * n : 2 * n + 1, :]
         cut = slice(n * LANES, (n + 1) * LANES)
@@ -181,30 +181,38 @@
         right[LANES:, cut] = table
         owner = lax.shift_right_logical(index, 14)
         chip = lax.shift_right_logical(owner, 3) * 4 + (owner & 3)
-        signs[:, cut] = sign_table(chip, 6)
+        bits = [bit_sign(chip, b) for b in range(6)]
+        spread.append([jnp.broadcast_to(bit, (COLS, LANES)) for bit in bits])
         factor = bit_sign(owner & (core * 4), 2)
         for b in range(6):
             if FIRST >> b & 1:
-                factor = factor * bit_sign(chip, b)
+                factor = factor * bits[b]
         factors.append(factor)
     answers = []
     width = 256
     for half in range(HALVES):
         for n in range(PICKS // 2 // width):
             cut = slice(half * PICKS // 2 + n * width, half * PICKS // 2 + (n + 1) * width)
-            total = jnp.zeros((COLS, width), jnp.float32)
-            for m in range(2):
+            stacks = [[] for _ in range(width // LANES)]
+            for m in range(4):
                 part = jnp.dot(
-                    left[half, m * 256 : (m + 1) * 256, :], right[:, cut], preferred_element_type=jnp.float32
+                    left[half, m * 128 : (m + 1) * 128, :], right[:, cut], preferred_element_type=jnp.float32
                 )
-                for j in range(32):
-                    total = total + part[j * COLS : (j + 1) * COLS, :] * signs[m * 32 + j : m * 32 + j + 1, cut]
-            answers += [total[:, :LANES], total[:, LANES:]]
+                for j in range(16):
+                    for i, stack in enumerate(stacks):
+                        tile = part[j * COLS : (j + 1) * COLS, i * LANES : (i + 1) * LANES]
+                        signs = spread[(half * 2 + n) * 2 + i]
+                        b = 0
+                        while (m * 16 + j) >> b & 1:
+                            tile = stack.pop() + tile * signs[b]
+                            b += 1
+                        stack.append(tile)
+            answers += [stack[0] for stack in stacks]
     answers = jnp.concatenate([answer * factor for answer, factor in zip(answers, factors)], axis=0)
     reply[...] = jnp.concatenate([answers, pltpu.roll(answers, CHIPS, 1)], axis=0).T[:CHIPS]
 
 
-def answer_other_kernel(message, reply, left, right, signs):
+def answer_other_kernel(message, reply, left, right):
     for half in range(HALVES):
         for pair in range(CHIPS // 2):
             tile = jnp.concatenate(
@@ -213,11 +221,11 @@
             high, low = split(tile)
             left[half, pl.ds(pair * 16, 16), :LANES] = high
             left[half, pl.ds(pair * 16, 16), LANES:] = low
-    answer(message, 1, left, reply, right, signs)
-
-
-def answer_own_kernel(message, left, reply, right, signs):
-    answer(message, 0, left, reply, right, signs)
+    answer(message, 1, left, reply, right)
+
+
+def answer_own_kernel(message, left, reply, right):
+    answer(message, 0, left, reply, right)
 
 
 def finish_kernel(reply, slots, sketch_hbm, gram_hbm, sketch, gram, sent):
@@ -292,7 +300,7 @@
     )(matrix, flips, own, owners_other, offsets_other)
     message = exchange(message, FIRST)
     reply_shape = jax.ShapeDtypeStruct((CHIPS, LANES), f32)
-    tables = [pltpu.VMEM((2 * LANES, PICKS), jnp.bfloat16), pltpu.VMEM((CHIPS, PICKS), f32)]
+    tables = [pltpu.VMEM((2 * LANES, PICKS), jnp.bfloat16)]
     theirs, left = pl.pallas_call(
         answer_other_kernel,
         name="answer_other",

time: 39.9 us -> 39.9 us (level)
  no operation moved by 1% of the time
where the time goes in v9:
time: 39.9 us; the launch traced here: 39.4 us
  blocking collectives  31 us (78%)
  Pallas kernels  4.27 us (11%)
  starting transfers between devices  3.22 us (8%)
  between operations  0.67 us (2%)
    all_to_all x2, blocking collectives, exchange(): lax.all_to_all(parts, 'all', split_axis=0, concat_axis=0, tiled=True, axi...  31 us
    ppermute x3, starting transfers between devices, other_core(): return lax.ppermute(value, 'all', [(i, i ^ 4) for i in range(2 * CHIPS)])  3.22 us
    pallas_call x1, Pallas kernels, on_device(): pl.pallas_call(load_kernel, name='load_and_requests', out_shape=(jax.Shap...  1.25 us
    pallas_call x1, Pallas kernels, on_device(): pl.pallas_call(finish_kernel, name='finish', out_shape=(jax.ShapeDtypeStr...  0.93 us
  transfers between devices with their start and end apart: 3, of which 1 were waited for; matrix products, arithmetic and copies ran while one was open for 0% of the time, Pallas kernels for 5%

profile of v9, /device:TPU:1, one launch (start us, length us, event | category | flops | bytes accessed | tf_op | source)
XLA Modules:
  0.0 39.4 jit_solution(12653428439800972082)
XLA Ops:
  0.6 1.5 %collective-permute-start = (s32[1,1024]{1,0:T(1,128)}, s32[1,1024]{1,0:T(1,128)S(1)}, u32[]{:S(2)}, u32[]{:S(2)}) collective-permute-start(s32[1,1024]{1,0:T(1,128)} %bitcast.16), channel_id=1, source_target_pairs={{0,4},{1,5},{2,6},{3,7},{4,0},{5,1},{6,2},{7,3},{8,12},{9,13},{10,... | collective-permute-start | bytes 12296 | tf_op jit(solution)/shard_map/ppermute | solution.py:37
  2.1 0.1 collective-permute-start.1
  2.2 1.2 %load_and_requests.1 = (f32[8,16384]{1,0:T(8,128)S(1)}, s32[128,128]{1,0:T(8,128)S(1)}, f32[16,128]{1,0:T(8,128)S(1)}, s32[1,1024]{1,0:T(1,128)S(1)}) custom-call(f32[8,16384]{1,0:T(8,128)} %matrix_hbm.1, s32[128,128]{1,0:T(8,128)} %bitcast.15, s32[1,1024]{1,0:T(1,128)} %bitcast.17, s32[1,1024]{1,0:T(1,128)} %bitcast.19), custom_call_target="tpu_custom_call" | custom-call | flops 4194304 | bytes 4194304 | tf_op jit(solution)/shard_map/load_and_requests/pallas_call | solution.py:268
  3.5 0.0 collective-permute-done.owners
  3.5 0.0 collective-permute-done.1.offsets
  3.5 0.7 %transform_and_requests.1 = f32[1088,128]{1,0:T(8,128)S(1)} custom-call(f32[8,16384]{1,0:T(8,128)S(1)} %get-tuple-element.10.matrix, s32[128,128]{1,0:T(8,128)S(1)} %get-tuple-element.11.flips, f32[16,128]{1,0:T(8,128)S(1)} %get-tuple-element.12.own, s32[1,1024]{1,0:T(1,128)S(1)} %collective-permute-done.owners, s32[1,1024]{1,0:T(1,128)S(1)} %collective-permute-done.1.offsets), custom_call_target="tpu_custom_call" | custom-call | tf_op jit(solution)/shard_map/transform_and_requests/pallas_call | solution.py:292
  4.2 19.1 %all_to_all.10 = f32[64,1,2176]{2,1,0:T(1,128)S(1)} all-to-all(f32[64,1,2176]{2,1,0:T(1,128)S(1)} %bitcast.12), channel_id=1, replica_groups={{90,91,88,89,82,83,80,81,74,75,72,73,66,67,64,65,122,123,120,121,114,11..., dimensions={0} | all-to-all | bytes 1114112 | tf_op jit(solution)/shard_map/all_to_all | solution.py:32
  23.3 0.7 %answer_other.1 = (f32[64,128]{1,0:T(8,128)S(1)}, bf16[2,512,256]{2,1,0:T(8,128)(2,1)S(1)}) custom-call(f32[1088,128]{1,0:T(8,128)S(1)} %bitcast.10), custom_call_target="tpu_custom_call" | custom-call | tf_op jit(solution)/shard_map/answer_other/pallas_call | solution.py:304
  24.1 1.6 %collective-permute-start.2 = (f32[64,128]{1,0:T(8,128)S(1)}, f32[64,128]{1,0:T(8,128)S(1)}, u32[]{:S(2)}, u32[]{:S(2)}) collective-permute-start(f32[64,128]{1,0:T(8,128)S(1)} %get-tuple-element.14), channel_id=1, source_target_pairs={{0,4},{1,5},{2,6},{3,7},{4,0},{5,1},{6,2},{7,3},{8,12},{9,13},{10,... | collective-permute-start | bytes 98312 | tf_op jit(solution)/shard_map/ppermute | solution.py:37
  25.7 0.7 %answer_own.1 = f32[64,128]{1,0:T(8,128)S(1)} custom-call(f32[1088,128]{1,0:T(8,128)S(1)} %bitcast.11, bf16[2,512,256]{2,1,0:T(8,128)(2,1)S(1)} %get-tuple-element.13.left), custom_call_target="tpu_custom_call" | custom-call | flops 268435456 | bytes 2097152 | tf_op jit(solution)/shard_map/answer_own/pallas_call | solution.py:314
  26.4 0.2 collective-permute-done.2
  26.5 11.9 %all_to_all.11 = f32[64,1,128]{2,1,0:T(1,128)S(1)} all-to-all(f32[64,1,128]{2,1,0:T(1,128)S(1)} %bitcast.14), channel_id=1, replica_groups={{82,83,80,81,90,91,88,89,66,67,64,65,74,75,72,73,114,115,112,113,122,12..., dimensions={0} | all-to-all | bytes 65536 | tf_op jit(solution)/shard_map/all_to_all | solution.py:32
  38.5 0.9 %finish.1 = (f32[8,1024]{1,0:T(8,128)}, f32[1,64]{1,0:T(1,128)}) custom-call(f32[64,128]{1,0:T(8,128)S(1)} %bitcast.13, s32[1,1024]{1,0:T(1,128)S(1)} %get-tuple-element.15.slots), custom_call_target="tpu_custom_call" | custom-call | tf_op jit(solution)/shard_map/finish/pallas_call | solution.py:325
  (1 shorter events, 0.0 us)
Async XLA Ops:
  0.6 2.9 %collective-permute-start = (s32[1,1024]{1,0:T(1,128)}, s32[1,1024]{1,0:T(1,128)S(1)}, u32[]{:S(2)}, u32[]{:S(2)}) collective-permute-start(s32[1,1024]{1,0:T(1,128)} %bitcast.16), channel_id=1, source_target_pairs={{0,4},{1,5},{2,6},{3,7},{4,0},{5,1},{6,2},{7,3},{8,12},{9,13},{10,... | collective-permute-start | bytes 12296 | tf_op jit(solution)/shard_map/ppermute | solution.py:37
  2.1 1.4 %collective-permute-start.1 = (s32[1,1024]{1,0:T(1,128)}, s32[1,1024]{1,0:T(1,128)S(1)}, u32[]{:S(2)}, u32[]{:S(2)}) collective-permute-start(s32[1,1024]{1,0:T(1,128)} %bitcast.18), channel_id=1, source_target_pairs={{0,4},{1,5},{2,6},{3,7},{4,0},{5,1},{6,2},{7,3},{8,12},{9,13},{10,... | collective-permute-start | bytes 12296 | tf_op jit(solution)/shard_map/ppermute | solution.py:37
  24.1 2.5 %collective-permute-start.2 = (f32[64,128]{1,0:T(8,128)S(1)}, f32[64,128]{1,0:T(8,128)S(1)}, u32[]{:S(2)}, u32[]{:S(2)}) collective-permute-start(f32[64,128]{1,0:T(8,128)S(1)} %get-tuple-element.14), channel_id=1, source_target_pairs={{0,4},{1,5},{2,6},{3,7},{4,0},{5,1},{6,2},{7,3},{8,12},{9,13},{10,... | collective-permute-start | bytes 98312 | tf_op jit(solution)/shard_map/ppermute | solution.py:37

commit v10 on v9

--- a/solution.py
+++ b/solution.py
@@ -15,7 +15,7 @@
 COLS = 8
 CHUNK = HALVES * COLS + 1
 PICKS = LANES * SLOTS
-PIECES = 1
+PIECES = 4
 FIRST = 46
 FIRST_BACK = 42
 VMEM = pl.BlockSpec(memory_space=pltpu.VMEM)
@@ -108,7 +108,7 @@
     for p in range(PIECES):
         cut = pl.ds(p * width, width)
         copies.append(pltpu.make_async_copy(matrix_hbm.at[:, cut], matrix.at[:, cut], arrived.at[3 + p]))
-    for copy in copies[2:0:-1] + copies[3:] + copies[:1]:
+    for copy in copies:
         copy.start()
     copies[1].wait()
     copies[2].wait()
@@ -125,9 +125,9 @@
 
 def send_kernel(matrix, flips, own, owners, offsets, message, mid):
     _, rows = requests(offsets[...], owners[...])
-    rest = jnp.zeros((CHIPS, LANES - 2 * HALVES * SLOTS), jnp.float32)
-    rows = jnp.concatenate([own[...], rows], axis=0).T[:CHIPS]
-    message[pl.ds(CHUNK - 1, CHIPS, stride=CHUNK), :] = jnp.concatenate([rows, rest], axis=1)
+    rest = jnp.zeros((LANES - 2 * HALVES * SLOTS, LANES), jnp.float32)
+    rows = jnp.concatenate([own[...], rows, rest], axis=0).T
+    message[pl.ds(CHUNK - 1, CHIPS, stride=CHUNK), :] = rows[:CHIPS]
     scale = 1.0 / math.sqrt(float(LANES) ** 3)
     signs = jnp.where(flips[...] == 1, scale, -scale)
     for i in range(16):

time: 39.9 us -> 40 us (level)
  no operation moved by 1% of the time
where the time goes in v10:
time: 40 us; the launch traced here: 39.4 us
  blocking collectives  31.1 us (78%)
  Pallas kernels  4.33 us (11%)
  starting transfers between devices  3.21 us (8%)
  between operations  0.68 us (2%)
    all_to_all x2, blocking collectives, exchange(): lax.all_to_all(parts, 'all', split_axis=0, concat_axis=0, tiled=True, axi...  31.1 us
    ppermute x3, starting transfers between devices, other_core(): return lax.ppermute(value, 'all', [(i, i ^ 4) for i in range(2 * CHIPS)])  3.21 us
    pallas_call x1, Pallas kernels, on_device(): pl.pallas_call(load_kernel, name='load_and_requests', out_shape=(jax.Shap...  1.31 us
    pallas_call x1, Pallas kernels, on_device(): pl.pallas_call(finish_kernel, name='finish', out_shape=(jax.ShapeDtypeStr...  0.93 us
  transfers between devices with their start and end apart: 3, of which 1 were waited for; matrix products, arithmetic and copies ran while one was open for 0% of the time, Pallas kernels for 5%

profile of v10, /device:TPU:1, one launch (start us, length us, event | category | flops | bytes accessed | tf_op | source)
XLA Modules:
  0.0 39.4 jit_solution(17595269561408528518)
XLA Ops:
  0.6 1.5 %collective-permute-start = (s32[1,1024]{1,0:T(1,128)}, s32[1,1024]{1,0:T(1,128)S(1)}, u32[]{:S(2)}, u32[]{:S(2)}) collective-permute-start(s32[1,1024]{1,0:T(1,128)} %bitcast.16), channel_id=1, source_target_pairs={{0,4},{1,5},{2,6},{3,7},{4,0},{5,1},{6,2},{7,3},{8,12},{9,13},{10,... | collective-permute-start | bytes 12296 | tf_op jit(solution)/shard_map/ppermute | solution.py:37
  2.1 0.1 collective-permute-start.1
  2.2 1.3 %load_and_requests.1 = (f32[8,16384]{1,0:T(8,128)S(1)}, s32[128,128]{1,0:T(8,128)S(1)}, f32[16,128]{1,0:T(8,128)S(1)}, s32[1,1024]{1,0:T(1,128)S(1)}) custom-call(f32[8,16384]{1,0:T(8,128)} %matrix_hbm.1, s32[128,128]{1,0:T(8,128)} %bitcast.15, s32[1,1024]{1,0:T(1,128)} %bitcast.17, s32[1,1024]{1,0:T(1,128)} %bitcast.19), custom_call_target="tpu_custom_call" | custom-call | flops 4194304 | bytes 4194304 | tf_op jit(solution)/shard_map/load_and_requests/pallas_call | solution.py:268
  3.5 0.0 collective-permute-done.owners
  3.6 0.0 collective-permute-done.1.offsets
  3.6 0.7 %transform_and_requests.1 = f32[1088,128]{1,0:T(8,128)S(1)} custom-call(f32[8,16384]{1,0:T(8,128)S(1)} %get-tuple-element.10.matrix, s32[128,128]{1,0:T(8,128)S(1)} %get-tuple-element.11.flips, f32[16,128]{1,0:T(8,128)S(1)} %get-tuple-element.12.own, s32[1,1024]{1,0:T(1,128)S(1)} %collective-permute-done.owners, s32[1,1024]{1,0:T(1,128)S(1)} %collective-permute-done.1.offsets), custom_call_target="tpu_custom_call" | custom-call | tf_op jit(solution)/shard_map/transform_and_requests/pallas_call | solution.py:292
  4.2 19.1 %all_to_all.10 = f32[64,1,2176]{2,1,0:T(1,128)S(1)} all-to-all(f32[64,1,2176]{2,1,0:T(1,128)S(1)} %bitcast.12), channel_id=1, replica_groups={{90,91,88,89,82,83,80,81,74,75,72,73,66,67,64,65,122,123,120,121,114,11..., dimensions={0} | all-to-all | bytes 1114112 | tf_op jit(solution)/shard_map/all_to_all | solution.py:32
  23.4 0.7 %answer_other.1 = (f32[64,128]{1,0:T(8,128)S(1)}, bf16[2,512,256]{2,1,0:T(8,128)(2,1)S(1)}) custom-call(f32[1088,128]{1,0:T(8,128)S(1)} %bitcast.10), custom_call_target="tpu_custom_call" | custom-call | tf_op jit(solution)/shard_map/answer_other/pallas_call | solution.py:304
  24.1 1.6 %collective-permute-start.2 = (f32[64,128]{1,0:T(8,128)S(1)}, f32[64,128]{1,0:T(8,128)S(1)}, u32[]{:S(2)}, u32[]{:S(2)}) collective-permute-start(f32[64,128]{1,0:T(8,128)S(1)} %get-tuple-element.14), channel_id=1, source_target_pairs={{0,4},{1,5},{2,6},{3,7},{4,0},{5,1},{6,2},{7,3},{8,12},{9,13},{10,... | collective-permute-start | bytes 98312 | tf_op jit(solution)/shard_map/ppermute | solution.py:37
  25.7 0.7 %answer_own.1 = f32[64,128]{1,0:T(8,128)S(1)} custom-call(f32[1088,128]{1,0:T(8,128)S(1)} %bitcast.11, bf16[2,512,256]{2,1,0:T(8,128)(2,1)S(1)} %get-tuple-element.13.left), custom_call_target="tpu_custom_call" | custom-call | flops 268435456 | bytes 2097152 | tf_op jit(solution)/shard_map/answer_own/pallas_call | solution.py:314
  26.4 0.2 collective-permute-done.2
  26.6 11.9 %all_to_all.11 = f32[64,1,128]{2,1,0:T(1,128)S(1)} all-to-all(f32[64,1,128]{2,1,0:T(1,128)S(1)} %bitcast.14), channel_id=1, replica_groups={{82,83,80,81,90,91,88,89,66,67,64,65,74,75,72,73,114,115,112,113,122,12..., dimensions={0} | all-to-all | bytes 65536 | tf_op jit(solution)/shard_map/all_to_all | solution.py:32
  38.5 0.9 %finish.1 = (f32[8,1024]{1,0:T(8,128)}, f32[1,64]{1,0:T(1,128)}) custom-call(f32[64,128]{1,0:T(8,128)S(1)} %bitcast.13, s32[1,1024]{1,0:T(1,128)S(1)} %get-tuple-element.15.slots), custom_call_target="tpu_custom_call" | custom-call | tf_op jit(solution)/shard_map/finish/pallas_call | solution.py:325
  (1 shorter events, 0.0 us)
Async XLA Ops:
  0.6 2.9 %collective-permute-start = (s32[1,1024]{1,0:T(1,128)}, s32[1,1024]{1,0:T(1,128)S(1)}, u32[]{:S(2)}, u32[]{:S(2)}) collective-permute-start(s32[1,1024]{1,0:T(1,128)} %bitcast.16), channel_id=1, source_target_pairs={{0,4},{1,5},{2,6},{3,7},{4,0},{5,1},{6,2},{7,3},{8,12},{9,13},{10,... | collective-permute-start | bytes 12296 | tf_op jit(solution)/shard_map/ppermute | solution.py:37
  2.1 1.4 %collective-permute-start.1 = (s32[1,1024]{1,0:T(1,128)}, s32[1,1024]{1,0:T(1,128)S(1)}, u32[]{:S(2)}, u32[]{:S(2)}) collective-permute-start(s32[1,1024]{1,0:T(1,128)} %bitcast.18), channel_id=1, source_target_pairs={{0,4},{1,5},{2,6},{3,7},{4,0},{5,1},{6,2},{7,3},{8,12},{9,13},{10,... | collective-permute-start | bytes 12296 | tf_op jit(solution)/shard_map/ppermute | solution.py:37
  24.1 2.5 %collective-permute-start.2 = (f32[64,128]{1,0:T(8,128)S(1)}, f32[64,128]{1,0:T(8,128)S(1)}, u32[]{:S(2)}, u32[]{:S(2)}) collective-permute-start(f32[64,128]{1,0:T(8,128)S(1)} %get-tuple-element.14), channel_id=1, source_target_pairs={{0,4},{1,5},{2,6},{3,7},{4,0},{5,1},{6,2},{7,3},{8,12},{9,13},{10,... | collective-permute-start | bytes 98312 | tf_op jit(solution)/shard_map/ppermute | solution.py:37

commit v11 on v7

--- a/solution.py
+++ b/solution.py
@@ -15,7 +15,7 @@
 COLS = 8
 CHUNK = HALVES * COLS + 1
 PICKS = LANES * SLOTS
-PIECES = 4
+PIECES = 2
 FIRST = 46
 FIRST_BACK = 42
 VMEM = pl.BlockSpec(memory_space=pltpu.VMEM)

time: 40 us -> 40 us (level)
  no operation moved by 1% of the time
where the time goes in v11:
time: 40 us; the launch traced here: 39.4 us
  blocking collectives  31 us (78%)
  Pallas kernels  4.35 us (11%)
  starting transfers between devices  3.21 us (8%)
  between operations  0.68 us (2%)
    all_to_all x2, blocking collectives, exchange(): lax.all_to_all(parts, 'all', split_axis=0, concat_axis=0, tiled=True, axi...  31 us
    ppermute x3, starting transfers between devices, other_core(): return lax.ppermute(value, 'all', [(i, i ^ 4) for i in range(2 * CHIPS)])  3.21 us
    pallas_call x1, Pallas kernels, on_device(): pl.pallas_call(load_kernel, name='load_and_requests', out_shape=(jax.Shap...  1.29 us
    pallas_call x1, Pallas kernels, on_device(): pl.pallas_call(finish_kernel, name='finish', out_shape=(jax.ShapeDtypeStr...  0.93 us
  transfers between devices with their start and end apart: 3, of which 1 were waited for; matrix products, arithmetic and copies ran while one was open for 0% of the time, Pallas kernels for 5%

profile of v11, /device:TPU:1, one launch (start us, length us, event | category | flops | bytes accessed | tf_op | source)
XLA Modules:
  0.0 39.4 jit_solution(8904704875659049613)
XLA Ops:
  0.6 1.5 %collective-permute-start = (s32[1,1024]{1,0:T(1,128)}, s32[1,1024]{1,0:T(1,128)S(1)}, u32[]{:S(2)}, u32[]{:S(2)}) collective-permute-start(s32[1,1024]{1,0:T(1,128)} %bitcast.16), channel_id=1, source_target_pairs={{0,4},{1,5},{2,6},{3,7},{4,0},{5,1},{6,2},{7,3},{8,12},{9,13},{10,... | collective-permute-start | bytes 12296 | tf_op jit(solution)/shard_map/ppermute | solution.py:37
  2.1 0.1 collective-permute-start.1
  2.2 1.3 %load_and_requests.1 = (f32[8,16384]{1,0:T(8,128)S(1)}, s32[128,128]{1,0:T(8,128)S(1)}, f32[16,128]{1,0:T(8,128)S(1)}, s32[1,1024]{1,0:T(1,128)S(1)}) custom-call(f32[8,16384]{1,0:T(8,128)} %matrix_hbm.1, s32[128,128]{1,0:T(8,128)} %bitcast.15, s32[1,1024]{1,0:T(1,128)} %bitcast.17, s32[1,1024]{1,0:T(1,128)} %bitcast.19), custom_call_target="tpu_custom_call" | custom-call | flops 4194304 | bytes 4194304 | tf_op jit(solution)/shard_map/load_and_requests/pallas_call | solution.py:260
  3.5 0.0 collective-permute-done.owners
  3.5 0.0 collective-permute-done.1.offsets
  3.5 0.7 %transform_and_requests.1 = f32[1088,128]{1,0:T(8,128)S(1)} custom-call(f32[8,16384]{1,0:T(8,128)S(1)} %get-tuple-element.10.matrix, s32[128,128]{1,0:T(8,128)S(1)} %get-tuple-element.11.flips, f32[16,128]{1,0:T(8,128)S(1)} %get-tuple-element.12.own, s32[1,1024]{1,0:T(1,128)S(1)} %collective-permute-done.owners, s32[1,1024]{1,0:T(1,128)S(1)} %collective-permute-done.1.offsets), custom_call_target="tpu_custom_call" | custom-call | tf_op jit(solution)/shard_map/transform_and_requests/pallas_call | solution.py:284
  4.2 19.1 %all_to_all.10 = f32[64,1,2176]{2,1,0:T(1,128)S(1)} all-to-all(f32[64,1,2176]{2,1,0:T(1,128)S(1)} %bitcast.12), channel_id=1, replica_groups={{90,91,88,89,82,83,80,81,74,75,72,73,66,67,64,65,122,123,120,121,114,11..., dimensions={0} | all-to-all | bytes 1114112 | tf_op jit(solution)/shard_map/all_to_all | solution.py:32
  23.4 0.7 %answer_other.1 = (f32[64,128]{1,0:T(8,128)S(1)}, bf16[2,512,256]{2,1,0:T(8,128)(2,1)S(1)}) custom-call(f32[1088,128]{1,0:T(8,128)S(1)} %bitcast.10), custom_call_target="tpu_custom_call" | custom-call | tf_op jit(solution)/shard_map/answer_other/pallas_call | solution.py:296
  24.1 1.6 %collective-permute-start.2 = (f32[64,128]{1,0:T(8,128)S(1)}, f32[64,128]{1,0:T(8,128)S(1)}, u32[]{:S(2)}, u32[]{:S(2)}) collective-permute-start(f32[64,128]{1,0:T(8,128)S(1)} %get-tuple-element.14), channel_id=1, source_target_pairs={{0,4},{1,5},{2,6},{3,7},{4,0},{5,1},{6,2},{7,3},{8,12},{9,13},{10,... | collective-permute-start | bytes 98312 | tf_op jit(solution)/shard_map/ppermute | solution.py:37
  25.7 0.7 %answer_own.1 = f32[64,128]{1,0:T(8,128)S(1)} custom-call(f32[1088,128]{1,0:T(8,128)S(1)} %bitcast.11, bf16[2,512,256]{2,1,0:T(8,128)(2,1)S(1)} %get-tuple-element.13.left), custom_call_target="tpu_custom_call" | custom-call | flops 268435456 | bytes 2097152 | tf_op jit(solution)/shard_map/answer_own/pallas_call | solution.py:306
  26.4 0.1 collective-permute-done.2
  26.6 11.9 %all_to_all.11 = f32[64,1,128]{2,1,0:T(1,128)S(1)} all-to-all(f32[64,1,128]{2,1,0:T(1,128)S(1)} %bitcast.14), channel_id=1, replica_groups={{82,83,80,81,90,91,88,89,66,67,64,65,74,75,72,73,114,115,112,113,122,12..., dimensions={0} | all-to-all | bytes 65536 | tf_op jit(solution)/shard_map/all_to_all | solution.py:32
  38.5 0.9 %finish.1 = (f32[8,1024]{1,0:T(8,128)}, f32[1,64]{1,0:T(1,128)}) custom-call(f32[64,128]{1,0:T(8,128)S(1)} %bitcast.13, s32[1,1024]{1,0:T(1,128)S(1)} %get-tuple-element.15.slots), custom_call_target="tpu_custom_call" | custom-call | tf_op jit(solution)/shard_map/finish/pallas_call | solution.py:317
  (1 shorter events, 0.0 us)
Async XLA Ops:
  0.6 2.9 %collective-permute-start = (s32[1,1024]{1,0:T(1,128)}, s32[1,1024]{1,0:T(1,128)S(1)}, u32[]{:S(2)}, u32[]{:S(2)}) collective-permute-start(s32[1,1024]{1,0:T(1,128)} %bitcast.16), channel_id=1, source_target_pairs={{0,4},{1,5},{2,6},{3,7},{4,0},{5,1},{6,2},{7,3},{8,12},{9,13},{10,... | collective-permute-start | bytes 12296 | tf_op jit(solution)/shard_map/ppermute | solution.py:37
  2.1 1.4 %collective-permute-start.1 = (s32[1,1024]{1,0:T(1,128)}, s32[1,1024]{1,0:T(1,128)S(1)}, u32[]{:S(2)}, u32[]{:S(2)}) collective-permute-start(s32[1,1024]{1,0:T(1,128)} %bitcast.18), channel_id=1, source_target_pairs={{0,4},{1,5},{2,6},{3,7},{4,0},{5,1},{6,2},{7,3},{8,12},{9,13},{10,... | collective-permute-start | bytes 12296 | tf_op jit(solution)/shard_map/ppermute | solution.py:37
  24.1 2.5 %collective-permute-start.2 = (f32[64,128]{1,0:T(8,128)S(1)}, f32[64,128]{1,0:T(8,128)S(1)}, u32[]{:S(2)}, u32[]{:S(2)}) collective-permute-start(f32[64,128]{1,0:T(8,128)S(1)} %get-tuple-element.14), channel_id=1, source_target_pairs={{0,4},{1,5},{2,6},{3,7},{4,0},{5,1},{6,2},{7,3},{8,12},{9,13},{10,... | collective-permute-start | bytes 98312 | tf_op jit(solution)/shard_map/ppermute | solution.py:37
